TPU v7x, 32 devices: a whole 2x2x4 slice. The times are simulated.
32 devices in a mesh: seq: 8 (over z, x), row: 4 (over y, core).
Axes of the slice: x: 2, y: 2, z: 4, core: 2. Of those that a mesh axis runs over, the one named last changes fastest.
Arguments:
- block_input: bfloat16 [4, 1024, 1024], P('row', 'seq'), may hold values from -6 to 6
- cotangent: bfloat16 [4, 1024, 1024], P('row', 'seq'), may hold values from -6 to 6
- doc_starts: int32 [4, 8], P('row'), may hold values from 0 to 1023, as said below
- qkv_weight: bfloat16 [1024, 3072], P('seq'), may hold values from -0.1875 to 0.1875
- beta_weight: bfloat16 [1024, 8], P('seq'), may hold values from -0.1875 to 0.1875
- conv_weight: bfloat16 [4, 3072], P(None, 'seq'), may hold values from -3 to 3
- norm_gains: bfloat16 [2, 1024], P(None, 'seq'), may hold values from 0.25 to 1.75
- head_gain: bfloat16 [128], P('seq'), may hold values from 0.25 to 1.75
- out_weight: bfloat16 [1024, 1024], P('seq'), may hold values from -0.1875 to 0.1875
- gate_up_weight: bfloat16 [1024, 5632], P('seq'), may hold values from -0.1875 to 0.1875
- down_weight: bfloat16 [2816, 1024], P('seq'), may hold values from -0.109375 to 0.109375
Outputs:
- mixed: bfloat16 [4, 1024, 1024], P('row', 'seq')
- block_input_gradient: bfloat16 [4, 1024, 1024], P('row', 'seq')
- grad_qkv: float32 [1024, 3072], P('seq')
- grad_beta: float32 [1024, 8], P('seq')
- grad_conv: float32 [4, 3072], P(None, 'seq')
- grad_gains: float32 [2, 1024], P(None, 'seq')
- grad_head_gain: float32 [128], P('seq')
- grad_out: float32 [1024, 1024], P('seq')
- grad_gate_up: float32 [1024, 5632], P('seq')
- grad_down: float32 [2816, 1024], P('seq')
Inputs may be any that keep to these rules, and one draw needn't show every extreme that they name: `doc_starts`: in each row the starts are non-decreasing, the first is 0 and the last is 1024 - 1 (a document may be empty); one document begins among the row's first 128 tokens and ends among its last 128.
All inputs are finite; a program needn't handle non-finite values.
Results may differ from a plain program's by a relative error of at most 0.023.
Values may be sent and summed in bfloat16 or wider, within the bound.
No kernel may reach another device: no remote copies, remote signals or barrier semaphores. Data moves between devices by JAX's collectives and lax.ppermute only.
A program may use at most 256 MiB of HBM per device.

v0:
```python
import jax
import jax.numpy as jnp
from jax import lax
from jax.sharding import PartitionSpec as P

H = 8
DK = 128
GROUP = 64


EPS_NORM = 1e-06
EPS_HEAD = 1e-05
EPS_UNIT = 1e-06
HIGH = lax.Precision.HIGHEST


def shifted(block, axis, distance):
    devices = range(lax.axis_size(axis))
    route = [(i - distance, i) for i in devices if i - distance in devices]
    return lax.ppermute(block, axis, route)


def dotf(first_op, second_op):
    return jnp.matmul(first_op, second_op, precision=HIGH)


def swap_last(matrix):
    return jnp.swapaxes(matrix, -1, -2)


def tok_dot(first_op, second_op):
    return lax.dot_general(
        first_op, second_op, (((0,), (0,)), ((), ())), preferred_element_type=jnp.float32
    )


def back_dot(first_op, second_op):
    return lax.dot_general(
        first_op, second_op, (((1,), (1,)), ((), ())), preferred_element_type=jnp.float32
    )


def unit_inverse(lower):
    identity = jnp.eye(lower.shape[-1], dtype=lower.dtype)
    power = lower
    result = identity - lower
    for step_index in range(lower.shape[-1].bit_length() - 2):
        power = dotf(power, power)
        result = dotf(result, identity + power)
    return result


def doc_index(positions, starts):
    return jnp.sum((starts[None, :] <= positions[:, None]).astype(jnp.int32), axis=1) - 1


def root_mean_square_backward(grad_in, normed, inverse):
    return inverse * (grad_in - normed * jnp.mean(grad_in * normed, -1, keepdims=True))


def silu_back(grad_in, pre):
    sig = jax.nn.sigmoid(pre)
    return grad_in * sig * (1.0 + pre * (1.0 - sig))


def on_device(
    block_input,
    cotangent,
    doc_starts,
    qkv_weight,
    beta_weight,
    conv_weight,
    norm_gains,
    head_gain,
    out_weight,
    gate_up_weight,
    down_weight,
):
    token_rows = block_input[0].astype(jnp.float32)
    cot_low = cotangent[0]
    seq_len = token_rows.shape[0]
    width = token_rows.shape[1]
    n_groups = seq_len // GROUP
    scale = DK ** (-0.5)
    w_qkv, w_beta, w_conv, w_gains, w_head, w_out, w_gu, w_down = (
        lax.all_gather(qkv_weight, "seq", axis=0, tiled=True),
        lax.all_gather(beta_weight, "seq", axis=0, tiled=True),
        lax.all_gather(conv_weight, "seq", axis=1, tiled=True),
        lax.all_gather(norm_gains, "seq", axis=1, tiled=True),
        lax.all_gather(head_gain, "seq", axis=0, tiled=True),
        lax.all_gather(out_weight, "seq", axis=0, tiled=True),
        lax.all_gather(gate_up_weight, "seq", axis=0, tiled=True),
        lax.all_gather(down_weight, "seq", axis=0, tiled=True),
    )
    conv_f = w_conv.astype(jnp.float32)
    float_gains = w_gains.astype(jnp.float32)
    head_f = w_head.astype(jnp.float32)
    seq_count = lax.axis_size("seq")
    seq_place = lax.axis_index("seq")
    starts = doc_starts[0]
    positions = seq_place * seq_len + jnp.arange(seq_len, dtype=jnp.int32)
    doc = doc_index(positions, starts)
    rim = conv_f.shape[0] - 1
    rim_doc = doc_index(seq_place * seq_len - rim + jnp.arange(rim, dtype=jnp.int32), starts)
    first_inverse_norm = lax.rsqrt(jnp.mean(token_rows * token_rows, -1, keepdims=True) + EPS_NORM)
    normalized_input = token_rows * first_inverse_norm
    first_activation = (normalized_input * float_gains[0]).astype(jnp.bfloat16)
    proj = jnp.dot(first_activation, w_qkv, preferred_element_type=jnp.float32).astype(jnp.bfloat16)
    rates_tok = jax.nn.sigmoid(
        jnp.dot(first_activation, w_beta, preferred_element_type=jnp.float32)
    )
    rim_vals = shifted(proj[seq_len - rim :], "seq", 1)
    extended = jnp.concatenate([rim_vals, proj], 0).astype(jnp.float32)
    ext_doc = jnp.concatenate([rim_doc, doc])
    matches = [
        (ext_doc[rim - tap : rim - tap + seq_len] == doc).astype(jnp.float32)[:, None]
        for tap in range(rim + 1)
    ]
    pre = jnp.zeros((seq_len, extended.shape[1]), jnp.float32)
    for tap in range(rim + 1):
        pre = pre + conv_f[tap] * extended[rim - tap : rim - tap + seq_len] * matches[tap]
    act = jax.nn.silu(pre)
    q_raw = act[:, :width].reshape(seq_len, H, DK)
    k_raw = act[:, width : 2 * width].reshape(seq_len, H, DK)
    v_raw = act[:, 2 * width :].reshape(seq_len, H, DK)
    q_inv = lax.rsqrt(jnp.sum(q_raw * q_raw, -1, keepdims=True) + EPS_UNIT)
    k_inv = lax.rsqrt(jnp.sum(k_raw * k_raw, -1, keepdims=True) + EPS_UNIT)
    q_unit = q_raw * q_inv
    k_unit = k_raw * k_inv

    def to_groups(arr):
        return (
            arr.astype(jnp.bfloat16)
            .astype(jnp.float32)
            .reshape(n_groups, GROUP, H, DK)
            .transpose(0, 2, 1, 3)
        )

    scaled_q = to_groups(q_unit) * scale
    keys = to_groups(k_unit)
    values = to_groups(v_raw)
    rates = rates_tok.reshape(n_groups, GROUP, H).transpose(0, 2, 1)
    block_doc = doc.reshape(n_groups, GROUP)
    prev_doc = doc_index(
        seq_place * seq_len + jnp.arange(n_groups, dtype=jnp.int32) * GROUP - 1, starts
    )
    places = jnp.arange(GROUP)
    same = block_doc[:, :, None] == block_doc[:, None, :]
    strict = ((places[:, None] > places[None, :])[None] & same)[:, None].astype(jnp.float32)
    incl = ((places[:, None] >= places[None, :])[None] & same)[:, None].astype(jnp.float32)
    keep = (block_doc == prev_doc[:, None]).astype(jnp.float32)[:, None, :, None]
    tail = (block_doc == block_doc[:, -1:]).astype(jnp.float32)[:, None, :, None]
    whole = keep[:, 0, -1, 0]
    scaled = keys * rates[..., None]
    lower = jnp.einsum("nhid,nhjd->nhij", scaled, keys, precision=HIGH) * strict
    inverse = unit_inverse(lower)
    w_mat = dotf(inverse, scaled)
    base = dotf(inverse, values * rates[..., None])
    eye_heads = jnp.broadcast_to(jnp.eye(DK, dtype=jnp.float32), (H, DK, DK))
    zero_heads = jnp.zeros((H, DK, DK), jnp.float32)

    def chain_step(maps, inputs):
        c_keys, c_w, c_base, c_keep, c_tail, c_whole = inputs
        mixed_maps = dotf(c_w[None], maps)
        reduce_part = jnp.einsum(
            "hcd,shce->shde", c_keys * (c_tail * c_keep), mixed_maps, precision=HIGH
        )
        maps = c_whole * maps - reduce_part
        shift_add = jnp.einsum("hcd,hce->hde", c_keys * c_tail, c_base, precision=HIGH)
        return (jnp.stack([maps[0], maps[1] + shift_add]), None)

    block_maps, unused = lax.scan(
        chain_step, jnp.stack([eye_heads, zero_heads]), (keys, w_mat, base, keep, tail, whole)
    )
    every_map, every_shift = (
        lax.all_gather(block_maps[0][None].astype(jnp.bfloat16), "seq", axis=0, tiled=True).astype(
            jnp.float32
        ),
        lax.all_gather(block_maps[1][None].astype(jnp.bfloat16), "seq", axis=0, tiled=True).astype(
            jnp.float32
        ),
    )

    def apply_map(position, state):
        return jnp.where(
            position < seq_place, dotf(every_map[position], state) + every_shift[position], state
        )

    state_in = lax.fori_loop(0, seq_count, apply_map, zero_heads)

    def out_step(state, inputs):
        c_q, c_keys, c_w, c_base, c_keep, c_tail, c_whole, c_incl = inputs
        pseudo = c_base - c_keep * dotf(c_w, state)
        scores = jnp.einsum("hid,hjd->hij", c_q, c_keys, precision=HIGH) * c_incl
        output = c_keep * dotf(c_q, state) + dotf(scores, pseudo)
        new_state = c_whole * state + jnp.einsum(
            "hcd,hce->hde", c_keys * c_tail, pseudo, precision=HIGH
        )
        return (new_state, (output, state))

    last_state, (outputs, block_states) = lax.scan(
        out_step, state_in, (scaled_q, keys, w_mat, base, keep, tail, whole, incl)
    )
    mixed_o = outputs.transpose(0, 2, 1, 3).reshape(seq_len, H, DK)
    head_inv = lax.rsqrt(jnp.mean(mixed_o * mixed_o, -1, keepdims=True) + EPS_HEAD)
    ohat = mixed_o * head_inv
    act_two = (ohat * head_f).reshape(seq_len, width).astype(jnp.bfloat16)
    resid = token_rows + jnp.dot(act_two, w_out, preferred_element_type=jnp.float32)
    inv_two = lax.rsqrt(jnp.mean(resid * resid, -1, keepdims=True) + EPS_NORM)
    rhat = resid * inv_two
    act_three = (rhat * float_gains[1]).astype(jnp.bfloat16)
    gate_up = jnp.dot(act_three, w_gu, preferred_element_type=jnp.float32)
    hidden_units = gate_up.shape[1] // 2
    gate = gate_up[:, :hidden_units]
    up_part = gate_up[:, hidden_units:]
    act_four = (jax.nn.silu(gate) * up_part).astype(jnp.bfloat16)
    mixed = (resid + jnp.dot(act_four, w_down, preferred_element_type=jnp.float32)).astype(
        jnp.bfloat16
    )
    grad_down = tok_dot(act_four, cot_low)
    d_act_four = back_dot(cot_low, w_down)
    d_gate = silu_back(d_act_four * up_part, gate)
    d_up = d_act_four * jax.nn.silu(gate)
    d_gate_up = jnp.concatenate([d_gate, d_up], 1).astype(jnp.bfloat16)
    grad_gate_up = tok_dot(act_three, d_gate_up)
    d_act_three = back_dot(d_gate_up, w_gu)
    grad_gain_two = jnp.sum(d_act_three * rhat, 0)
    residual_gradient = cot_low.astype(jnp.float32) + root_mean_square_backward(
        d_act_three * float_gains[1], rhat, inv_two
    )
    d_resid_low = residual_gradient.astype(jnp.bfloat16)
    grad_out = tok_dot(act_two, d_resid_low)
    d_act_two = back_dot(d_resid_low, w_out).reshape(seq_len, H, DK)
    grad_head = jnp.sum(d_act_two * ohat, (0, 1))
    d_mixed_o = root_mean_square_backward(d_act_two * head_f, ohat, head_inv)
    d_out_groups = d_mixed_o.reshape(n_groups, GROUP, H, DK).transpose(0, 2, 1, 3)

    def state_grad(grad_state, inputs):
        c_q, c_keys, c_scaled, c_inverse, c_keep, c_tail, c_whole, c_incl, c_dout = inputs
        scores = jnp.einsum("hid,hjd->hij", c_q, c_keys, precision=HIGH) * c_incl
        d_pseudo = jnp.einsum("hij,hid->hjd", scores, c_dout, precision=HIGH) + c_tail * dotf(
            c_keys, grad_state
        )
        d_res = jnp.einsum("hij,hid->hjd", c_inverse, d_pseudo, precision=HIGH)
        prior = (
            jnp.einsum("hcd,hce->hde", c_q * c_keep, c_dout, precision=HIGH) + c_whole * grad_state
        )
        return (prior - jnp.einsum("hcd,hce->hde", c_scaled * c_keep, d_res, precision=HIGH), None)

    local_grad, unused = lax.scan(
        state_grad,
        zero_heads,
        (scaled_q, keys, scaled, inverse, keep, tail, whole, incl, d_out_groups),
        reverse=True,
    )
    back_maps = swap_last(block_maps[0])
    every_back, every_grad = (
        lax.all_gather(back_maps[None].astype(jnp.bfloat16), "seq", axis=0, tiled=True).astype(
            jnp.float32
        ),
        lax.all_gather(local_grad[None].astype(jnp.bfloat16), "seq", axis=0, tiled=True).astype(
            jnp.float32
        ),
    )

    def apply_back(step_index, grad_state):
        position = seq_count - 1 - step_index
        return jnp.where(
            position > seq_place,
            dotf(every_back[position], grad_state) + every_grad[position],
            grad_state,
        )

    grad_state_out = lax.fori_loop(0, seq_count, apply_back, zero_heads)

    def full_back(grad_state, inputs):
        (
            c_q,
            c_keys,
            c_values,
            c_rates,
            c_scaled,
            c_inverse,
            c_w,
            c_base,
            c_keep,
            c_tail,
            c_whole,
            c_strict,
            c_incl,
            c_dout,
            c_state,
        ) = inputs
        pseudo = c_base - c_keep * dotf(c_w, c_state)
        scores = jnp.einsum("hid,hjd->hij", c_q, c_keys, precision=HIGH) * c_incl
        d_pseudo = jnp.einsum("hij,hid->hjd", scores, c_dout, precision=HIGH) + c_tail * dotf(
            c_keys, grad_state
        )
        d_res = jnp.einsum("hij,hid->hjd", c_inverse, d_pseudo, precision=HIGH)
        prior = (
            jnp.einsum("hcd,hce->hde", c_q * c_keep, c_dout, precision=HIGH) + c_whole * grad_state
        )
        prior = prior - jnp.einsum("hcd,hce->hde", c_scaled * c_keep, d_res, precision=HIGH)
        d_scores = jnp.einsum("hid,hjd->hij", c_dout, pseudo, precision=HIGH) * c_incl
        d_query = c_keep * dotf(c_dout, swap_last(c_state)) + dotf(d_scores, c_keys)
        d_keys = jnp.einsum("hij,hid->hjd", d_scores, c_q, precision=HIGH) + c_tail * dotf(
            pseudo, swap_last(grad_state)
        )
        d_lower = -jnp.einsum("hid,hjd->hij", d_res, pseudo, precision=HIGH) * c_strict
        d_scaled = -c_keep * dotf(d_res, swap_last(c_state)) + dotf(d_lower, c_keys)
        d_keys = (
            d_keys
            + jnp.einsum("hij,hid->hjd", d_lower, c_scaled, precision=HIGH)
            + c_rates[..., None] * d_scaled
        )
        d_values = c_rates[..., None] * d_res
        d_rates = jnp.sum(d_res * c_values, -1) + jnp.sum(d_scaled * c_keys, -1)
        return (prior, (d_query * scale, d_keys, d_values, d_rates))

    first_grad, (d_q_groups, d_k_groups, d_v_groups, d_rate_groups) = lax.scan(
        full_back,
        grad_state_out,
        (
            scaled_q,
            keys,
            values,
            rates,
            scaled,
            inverse,
            w_mat,
            base,
            keep,
            tail,
            whole,
            strict,
            incl,
            d_out_groups,
            block_states,
        ),
        reverse=True,
    )

    def from_groups(arr):
        return arr.transpose(0, 2, 1, 3).reshape(seq_len, H, DK)

    d_q_unit = from_groups(d_q_groups)
    d_k_unit = from_groups(d_k_groups)
    d_q_raw = q_inv * (d_q_unit - q_unit * jnp.sum(d_q_unit * q_unit, -1, keepdims=True))
    d_k_raw = k_inv * (d_k_unit - k_unit * jnp.sum(d_k_unit * k_unit, -1, keepdims=True))
    d_act = jnp.concatenate(
        [
            d_q_raw.reshape(seq_len, width),
            d_k_raw.reshape(seq_len, width),
            from_groups(d_v_groups).reshape(seq_len, width),
        ],
        1,
    )
    d_pre = silu_back(d_act, pre)
    d_extended = jnp.zeros((seq_len + rim, d_pre.shape[1]), jnp.float32)
    conv_grads = []
    for tap in range(rim + 1):
        masked = d_pre * matches[tap]
        d_extended = d_extended + jnp.pad(conv_f[tap] * masked, ((rim - tap, tap), (0, 0)))
        conv_grads.append(jnp.sum(masked * extended[rim - tap : rim - tap + seq_len], 0))
    grad_conv = jnp.stack(conv_grads)
    rim_back = shifted(d_extended[:rim].astype(jnp.bfloat16), "seq", -1).astype(jnp.float32)
    d_proj = (d_extended[rim:] + jnp.pad(rim_back, ((seq_len - rim, 0), (0, 0)))).astype(
        jnp.bfloat16
    )
    d_rates_tok = d_rate_groups.transpose(0, 2, 1).reshape(seq_len, H)
    d_logits = (d_rates_tok * rates_tok * (1.0 - rates_tok)).astype(jnp.bfloat16)
    grad_qkv = tok_dot(first_activation, d_proj)
    grad_beta = tok_dot(first_activation, d_logits)
    first_activation_gradient = back_dot(d_proj, w_qkv) + back_dot(d_logits, w_beta)
    first_gain_gradient = jnp.sum(first_activation_gradient * normalized_input, 0)
    block_input_gradient = (
        residual_gradient
        + root_mean_square_backward(
            first_activation_gradient * float_gains[0], normalized_input, first_inverse_norm
        )
    ).astype(jnp.bfloat16)
    grad_gains = jnp.stack([first_gain_gradient, grad_gain_two])
    red_qkv, red_beta, red_conv, red_gains, red_head, red_out, red_gu, red_down = (
        lax.psum_scatter(
            grad_qkv.astype(jnp.bfloat16), "seq", scatter_dimension=0, tiled=True
        ).astype(jnp.float32),
        lax.psum_scatter(
            grad_beta.astype(jnp.bfloat16), "seq", scatter_dimension=0, tiled=True
        ).astype(jnp.float32),
        lax.psum_scatter(
            grad_conv.astype(jnp.bfloat16), "seq", scatter_dimension=1, tiled=True
        ).astype(jnp.float32),
        lax.psum_scatter(
            grad_gains.astype(jnp.bfloat16), "seq", scatter_dimension=1, tiled=True
        ).astype(jnp.float32),
        lax.psum_scatter(
            grad_head.astype(jnp.bfloat16), "seq", scatter_dimension=0, tiled=True
        ).astype(jnp.float32),
        lax.psum_scatter(
            grad_out.astype(jnp.bfloat16), "seq", scatter_dimension=0, tiled=True
        ).astype(jnp.float32),
        lax.psum_scatter(
            grad_gate_up.astype(jnp.bfloat16), "seq", scatter_dimension=0, tiled=True
        ).astype(jnp.float32),
        lax.psum_scatter(
            grad_down.astype(jnp.bfloat16), "seq", scatter_dimension=0, tiled=True
        ).astype(jnp.float32),
    )
    red_qkv, red_beta, red_conv, red_gains, red_head, red_out, red_gu, red_down = (
        lax.psum(red_qkv.astype(jnp.bfloat16), "row").astype(jnp.float32),
        lax.psum(red_beta.astype(jnp.bfloat16), "row").astype(jnp.float32),
        lax.psum(red_conv.astype(jnp.bfloat16), "row").astype(jnp.float32),
        lax.psum(red_gains.astype(jnp.bfloat16), "row").astype(jnp.float32),
        lax.psum(red_head.astype(jnp.bfloat16), "row").astype(jnp.float32),
        lax.psum(red_out.astype(jnp.bfloat16), "row").astype(jnp.float32),
        lax.psum(red_gu.astype(jnp.bfloat16), "row").astype(jnp.float32),
        lax.psum(red_down.astype(jnp.bfloat16), "row").astype(jnp.float32),
    )
    return (
        mixed[None],
        block_input_gradient[None],
        red_qkv,
        red_beta,
        red_conv,
        red_gains,
        red_head,
        red_out,
        red_gu,
        red_down,
    )


def solution(mesh):
    in_specs = (
        P("row", "seq", None),
        P("row", "seq", None),
        P("row", None),
        P("seq", None),
        P("seq", None),
        P(None, "seq"),
        P(None, "seq"),
        P("seq"),
        P("seq", None),
        P("seq", None),
        P("seq", None),
    )
    out_specs = (
        P("row", "seq", None),
        P("row", "seq", None),
        P("seq", None),
        P("seq", None),
        P(None, "seq"),
        P(None, "seq"),
        P("seq"),
        P("seq", None),
        P("seq", None),
        P("seq", None),
    )
    return jax.shard_map(
        on_device, mesh=mesh, in_specs=in_specs, out_specs=out_specs, check_vma=False
    )
```

profile of v0, /device:TPU:0, one launch (start us, length us, event | category | flops | bytes accessed | tf_op | source)
XLA Modules:
  0.0 1435.5 jit_solution(3151335229972577218)
XLA Ops:
  8.9 22.4 %all_gather.37 = bf16[2,1024]{1,0:T(2,128)(2,1)S(1)} all-gather(bf16[2,128]{1,0:T(2,128)(2,1)} %param.29), channel_id=1, replica_groups=mesh['seq'=8,'row'=4] {'seq'}, dimensions={1}, use_global_device_ids=true | all-gather | bytes 4608 | tf_op jit(solution)/shard_map/all_gather | solution.py:89
  31.3 26.6 %all_gather.39 = bf16[1024,8]{0,1:T(8,128)(2,1)S(1)} all-gather(bf16[128,8]{0,1:T(8,128)(2,1)} %param.27), channel_id=1, replica_groups=mesh['seq'=8,'row'=4] {'seq'}, dimensions={0}, use_global_device_ids=true | all-gather | bytes 18432 | tf_op jit(solution)/shard_map/all_gather | solution.py:87
  57.8 31.1 %all_gather.36 = bf16[4,3072]{1,0:T(4,128)(2,1)S(1)} all-gather(bf16[4,384]{1,0:T(4,128)(2,1)} %param.28), channel_id=1, replica_groups=mesh['seq'=8,'row'=4] {'seq'}, dimensions={1}, use_global_device_ids=true | all-gather | bytes 27648 | tf_op jit(solution)/shard_map/all_gather | solution.py:88
  94.8 17.9 %all-gather.11.cloned.1.call-done = bf16[1024,3072]{1,0:T(8,128)(2,1)} async-done(((bf16[128,3072]{1,0:T(8,128)(2,1)}), bf16[1024,3072]{1,0:T(8,128)(2,1)}) %all-gather.11.cloned.1.call-update) | async-done | bytes 6291472 | tf_op jit(solution)/shard_map/all_gather | solution.py:86
  136.9 11.7 while.91
  153.9 20.5 %all-reduce.6 = bf16[128]{0:T(256)(128)(2,1)S(1)} all-reduce(bf16[128]{0:T(256)(128)(2,1)S(1)} %dynamic-update-slice), channel_id=1, replica_groups=mesh['seq'=8,'row'=4] {'seq'}, use_global_device_ids=true, to_apply=%add.6 | all-reduce | flops 128 | bytes 512
  186.9 13.3 all-gather.13.cloned.1.call-done
  204.3 46.4 %all-gather.15.cloned.1.call-done = bf16[8,8,128,128]{3,2,1,0:T(8,128)(2,1)} async-done(((bf16[1,8,128,128]{3,2,1,0:T(8,128)(2,1)}), bf16[8,8,128,128]{3,2,1,0:T(8,128)(2,1)}) %all-gather.15.cloned.1.call-update) | async-done | bytes 2097168 | tf_op jit(solution)/shard_map/all_gather | solution.py:179
  254.8 24.0 %while.94 = (s32[]{:T(128)}, f32[8,128,128]{2,1,0:T(8,128)S(1)}, s32[]{:T(128)}, f32[8,8,128,128]{3,2,1,0:T(8,128)}, f32[8,8,128,128]{3,2,1,0:T(8,128)}, /*index=5*/s32[]{:T(128)}, s32[]{:T(128)}) while((s32[]{:T(128)}, f32[8,128,128]{2,1,0:T(8,128)S(1)}, s32[]{:T(128)}, f32[8,8,128,128]{3,2,1,0:T(8,128)}, ...), condition=%wide.region_8.9_spmd.clone, body=%wide.region_7.8_spmd.clone.sunk | while | flops 201850880 | bytes 3672679 | solution.py:189
  278.8 12.5 while.92
  303.3 161.4 %all-gather.19.cloned.1.call-done = bf16[1024,5632]{1,0:T(8,128)(2,1)} async-done(((bf16[128,5632]{1,0:T(8,128)(2,1)}), bf16[1024,5632]{1,0:T(8,128)(2,1)}) %all-gather.19.cloned.1.call-update) | async-done | bytes 11534352 | tf_op jit(solution)/shard_map/all_gather | solution.py:92
  472.3 85.3 %all-gather.21.cloned.1.call-done = bf16[2816,1024]{1,0:T(8,128)(2,1)} async-done(((bf16[352,1024]{1,0:T(8,128)(2,1)}), bf16[2816,1024]{1,0:T(8,128)(2,1)}) %all-gather.21.cloned.1.call-update) | async-done | bytes 5767184 | tf_op jit(solution)/shard_map/all_gather | solution.py:93
  582.2 14.0 while.95
  615.9 42.1 %all-gather.25.cloned.1.call-done = bf16[64,128,128]{2,1,0:T(8,128)(2,1)} async-done(((bf16[8,128,128]{2,1,0:T(8,128)(2,1)}), bf16[64,128,128]{2,1,0:T(8,128)(2,1)}) %all-gather.25.cloned.1.call-update) | async-done | bytes 2097168 | tf_op jit(solution)/shard_map/all_gather | solution.py:261
  662.1 24.3 %while.96 = (s32[]{:T(128)}, f32[8,128,128]{2,1,0:T(8,128)S(1)}, s32[]{:T(128)}, f32[8,8,128,128]{3,2,1,0:T(8,128)}, f32[8,8,128,128]{3,2,1,0:T(8,128)}, /*index=5*/s32[]{:T(128)}, s32[]{:T(128)}, s32[]{:T(128)}, s32[]{:T(128)}) while((s32[]{:T(128)}, f32[8,128,128]{2,1,0:T(8,128)S(1)}, s32[]{:T(128)}, ...), condition=%wide.region_19.20_spmd.clone, body=%wide.region_18.19_spmd.clone.sunk | while | flops 201850880 | bytes 3672741 | solution.py:274
  689.6 32.6 %while.93 = (s32[]{:T(128)}, f32[8,128,128]{2,1,0:T(8,128)S(1)}, f32[2,8,64,128]{3,2,1,0:T(8,128)}, f32[2,8,64,128]{3,2,1,0:T(8,128)}, f32[2,8,64,128]{3,2,1,0:T...) while((s32[]{:T(128)}, f32[8,128,128]{2,1,0:T(8,128)S(1)}, ...), condition=%wide.region_23.24_spmd, body=%wide.region_20.23_spmd.sunk | while | flops 1159527936 | bytes 35874440 | solution.py:320
  761.7 79.1 %reduce-scatter.20.cloned.1.call-done = bf16[352,1024]{1,0:T(8,128)(2,1)} async-done(((bf16[2816,1024]{1,0:T(8,128)(2,1)}), bf16[352,1024]{1,0:T(8,128)(2,1)}) %reduce-scatter.20.cloned.1.call-update) | async-done | bytes 720912 | tf_op jit(solution)/shard_map/reduce_scatter | solution.py:405
  840.8 121.4 %reduce-scatter.14.cloned.1.call-done = bf16[128,3072]{1,0:T(8,128)(2,1)} async-done(((bf16[1024,3072]{1,0:T(8,128)(2,1)}), bf16[128,3072]{1,0:T(8,128)(2,1)}) %reduce-scatter.14.cloned.1.call-update) | async-done | bytes 786448 | tf_op jit(solution)/shard_map/reduce_scatter | solution.py:384
  962.1 195.4 %reduce-scatter.18.cloned.1.call-done = bf16[128,5632]{1,0:T(8,128)(2,1)} async-done(((bf16[1024,5632]{1,0:T(8,128)(2,1)}), bf16[128,5632]{1,0:T(8,128)(2,1)}) %reduce-scatter.18.cloned.1.call-update) | async-done | bytes 1441808 | tf_op jit(solution)/shard_map/reduce_scatter | solution.py:402
  1158.3 19.4 %all-reduce.7 = bf16[128]{0:T(256)(128)(2,1)S(1)} all-reduce(bf16[128]{0:T(256)(128)(2,1)S(1)} %bitcast_reduce_fusion), channel_id=8, replica_groups=mesh['seq'=8,'row'=4] {'seq'}, use_global_device_ids=true, to_apply=%region_43.44.clone | all-reduce | flops 128 | bytes 512
  1183.1 38.0 %reduce-scatter.26.cloned.1.call-done = bf16[128,2]{1,0:T(8,128)(2,1)} async-done(((bf16[1024,2]{1,0:T(8,128)(2,1)}), bf16[128,2]{1,0:T(8,128)(2,1)}) %reduce-scatter.26.cloned.1.call-update) | async-done | bytes 528
  1222.0 63.2 %reduce-scatter.22.cloned.1.call-done = bf16[128,8]{1,0:T(8,128)(2,1)} async-done(((bf16[1024,8]{1,0:T(8,128)(2,1)}), bf16[128,8]{1,0:T(8,128)(2,1)}) %reduce-scatter.22.cloned.1.call-update) | async-done | bytes 2064
  1286.0 64.4 %reduce-scatter.24.cloned.1.call-done = bf16[384,4]{1,0:T(8,128)(2,1)} async-done(((bf16[3072,4]{1,0:T(8,128)(2,1)}), bf16[384,4]{1,0:T(8,128)(2,1)}) %reduce-scatter.24.cloned.1.call-update) | async-done | bytes 3088
  1359.4 62.8 %all-reduce.12.cloned.1.call-done = (bf16[128,3072]{1,0:T(8,128)(2,1)}, bf16[128,1024]{1,0:T(8,128)(2,1)}, bf16[128,5632]{1,0:T(8,128)(2,1)}, bf16[352,1024]{1,0:T(8,128)(2,1)}) async-done(((bf16[128,3072]{1,0:T(8,128)(2,1)}, bf16[128,1024]{1,0:T(8,128)(2,1)}, bf16[128,5632]{1,0:T(8,128)(2,1)}, bf16[352,1024]{1,0:T(8,128)(2,1)}), (bf16[128,3072]{1,0:T(8,128)(2,1)}, bf16[128,1024]{1,0:T(8,128)(2,1)}, ...) | async-done | bytes 3211280 | tf_op jit(solution)/shard_map/psum | solution.py:410
  (596 shorter events, 305.7 us)
Async XLA Ops:
  7.2 105.5 %copy-start.18 = (bf16[1,128,1024]{2,1,0:T(8,128)(2,1)S(1)}, bf16[1,128,1024]{2,1,0:T(8,128)(2,1)}, u32[]{:S(2)}) copy-start(bf16[1,128,1024]{2,1,0:T(8,128)(2,1)} %param.23) | copy-start | bytes 786436
  7.2 105.5 %all-gather.11.cloned.1.call-start = ((), (), s32[]{:S(2)}) async-start(), calls=%async_computation.7 | async-start | bytes 7077888 | tf_op jit(solution)/shard_map/all_gather | solution.py:86
  7.9 192.3 %all-gather.13.cloned.1.call-start = ((), (), s32[]{:S(2)}) async-start(), calls=%async_computation.8 | async-start | bytes 2359296 | tf_op jit(solution)/shard_map/all_gather | solution.py:176
  8.9 107.6 %copy-start.87 = (s32[2,64]{1,0:T(2,128)}, s32[2,64]{1,0:T(2,128)S(1)}, u32[]{:S(2)}) copy-start(s32[2,64]{1,0:T(2,128)S(1)} %sub.129) | copy-start | bytes 1540
  57.8 58.7 %copy-start.76 = (bf16[1024,8]{0,1:T(8,128)(2,1)}, bf16[1024,8]{0,1:T(8,128)(2,1)S(1)}, u32[]{:S(2)}) copy-start(bf16[1024,8]{0,1:T(8,128)(2,1)S(1)} %all_gather.39) | copy-start | bytes 49156
  90.1 26.4 %copy-start.72 = (pred[64,64]{1,0:T(8,128)(4,1)}, pred[64,64]{1,0:T(8,128)(4,1)S(1)}, u32[]{:S(2)}) copy-start(pred[64,64]{1,0:T(8,128)(4,1)S(1)} %iota_compare_fusion.2) | copy-start | bytes 12292
  94.1 25.8 %copy-start.91 = (f32[128,8]{0,1:T(8,128)}, f32[128,8]{0,1:T(8,128)S(1)}, u32[]{:S(2)}) copy-start(f32[128,8]{0,1:T(8,128)S(1)} %fusion.153) | copy-start | bytes 12292
  116.6 4.0 collective-permute-start
  149.8 101.0 %all-gather.15.cloned.1.call-start = ((), (), s32[]{:S(2)}) async-start(), calls=%async_computation.9 | async-start | bytes 2359296 | tf_op jit(solution)/shard_map/all_gather | solution.py:179
  150.5 150.0 %all-gather.17.cloned.1.call-start = ((), (), s32[]{:S(2)}) async-start(), calls=%async_computation.10 | async-start | bytes 2359296 | tf_op jit(solution)/shard_map/all_gather | solution.py:91
  151.1 313.6 %all-gather.19.cloned.1.call-start = ((), (), s32[]{:S(2)}) async-start(), calls=%async_computation.11 | async-start | bytes 12976128 | tf_op jit(solution)/shard_map/all_gather | solution.py:92
  151.7 405.9 %all-gather.21.cloned.1.call-start = ((), (), s32[]{:S(2)}) async-start(), calls=%async_computation.12 | async-start | bytes 6488064 | tf_op jit(solution)/shard_map/all_gather | solution.py:93
  152.3 455.1 %all-gather.23.cloned.1.call-start = ((), (), s32[]{:S(2)}) async-start(), calls=%async_computation.17 | async-start | bytes 2359296 | tf_op jit(solution)/shard_map/all_gather | solution.py:258
  186.8 471.1 %all-gather.25.cloned.1.call-start = ((), (), s32[]{:S(2)}) async-start(), calls=%async_computation.18 | async-start | bytes 2359296 | tf_op jit(solution)/shard_map/all_gather | solution.py:261
  302.7 268.8 %copy-start.9 = (f32[128,1024]{1,0:T(8,128)}, f32[128,1024]{1,0:T(8,128)S(1)}, u32[]{:S(2)}) copy-start(f32[128,1024]{1,0:T(8,128)S(1)} %get-tuple-element.1552) | copy-start | bytes 1572868
  597.0 164.7 %reduce-scatter.16.cloned.1.call-start = ((), (), s32[]{:S(2)}) async-start(), calls=%async_computation.14 | async-start | bytes 2359296 | tf_op jit(solution)/shard_map/reduce_scatter | solution.py:399
  600.2 240.5 %reduce-scatter.20.cloned.1.call-start = ((), (), s32[]{:S(2)}) async-start(), calls=%async_computation.16 | async-start | bytes 6488064 | tf_op jit(solution)/shard_map/reduce_scatter | solution.py:405
  615.8 346.3 %reduce-scatter.14.cloned.1.call-start = ((), (), s32[]{:S(2)}) async-start(), calls=%async_computation.13 | async-start | bytes 7077888 | tf_op jit(solution)/shard_map/reduce_scatter | solution.py:384
  732.4 5.7 collective-permute-start.1
  742.7 414.8 %reduce-scatter.18.cloned.1.call-start = ((), (), s32[]{:S(2)}) async-start(), calls=%async_computation.15 | async-start | bytes 12976128 | tf_op jit(solution)/shard_map/reduce_scatter | solution.py:402
  751.1 470.0 %reduce-scatter.26.cloned.1.call-start = ((), (), s32[]{:S(2)}) async-start(), calls=%async_computation.21 | async-start | bytes 294912
  759.0 526.2 %reduce-scatter.22.cloned.1.call-start = ((), (), s32[]{:S(2)}) async-start(), calls=%async_computation.19 | async-start | bytes 294912
  760.2 590.2 %reduce-scatter.24.cloned.1.call-start = ((), (), s32[]{:S(2)}) async-start(), calls=%async_computation.20 | async-start | bytes 884736
  761.6 660.6 %all-reduce.12.cloned.1.call-start = ((), (), s32[]{:S(2)}) async-start(), calls=%async_computation.22 | async-start | bytes 6422528 | tf_op jit(solution)/shard_map/psum | solution.py:410
  (122 other events, 406.5 us)
Sparse Core Ops, SparseCore 0:
  10.2 102.3 all-gather.10
  149.9 50.2 all-gather.12
  202.9 47.7 all-gather.14
  252.7 47.7 all-gather.16
  302.6 162.1 all-gather.18
  466.8 90.8 all-gather.20
  559.7 47.6 all-gather.22
  610.1 47.8 all-gather.24
  662.1 66.1 reduce-scatter.15
  731.8 108.9 reduce-scatter.19
  844.3 117.7 reduce-scatter.13
  965.6 191.8 reduce-scatter.17
  1160.8 60.3 reduce-scatter.25
  1224.9 60.2 reduce-scatter.21
  1288.9 61.4 reduce-scatter.23
  1353.1 69.0 all-reduce.11
where the time goes:
time: 1440 us
  waiting for transfers between devices  1000 us (69%)
  matrix products  157 us (11%)
  blocking collectives  126 us (9%)
  local copies, waits for them, and re-layouts  64.9 us (5%)
  other arithmetic  59.5 us (4%)
  between operations  16.9 us (1%)
    reduce_scatter x1, waiting for transfers between devices, on_device(): lax.psum_scatter(grad_gate_up.astype(jnp.bfloat16), 'seq', scatter_dimens...  195 us
    unnamed x19, waiting for transfers between devices  169 us
    all_gather x1, waiting for transfers between devices, on_device(): lax.all_gather(gate_up_weight, 'seq', axis=0, tiled=True)  161 us
    reduce_scatter x1, waiting for transfers between devices, on_device(): lax.psum_scatter(grad_qkv.astype(jnp.bfloat16), 'seq', scatter_dimension=...  121 us
    all_gather x1, waiting for transfers between devices, on_device(): lax.all_gather(down_weight, 'seq', axis=0, tiled=True)  85.3 us
    reduce_scatter x1, waiting for transfers between devices, on_device(): lax.psum_scatter(grad_down.astype(jnp.bfloat16), 'seq', scatter_dimension...  79.1 us
    psum x1, waiting for transfers between devices, on_device(): lax.psum(red_qkv.astype(jnp.bfloat16), 'row').astype(jnp.float32)  62.8 us
    dot_general x52, matrix products, dotf(): return jnp.matmul(first_op, second_op, precision=HIGH)  62.5 us
  transfers between devices with their start and end apart: 18, of which 17 were waited for; matrix products, arithmetic and copies ran while one was open for 16% of the time, Pallas kernels for 0%

commit v1 on v0

--- a/solution.py
+++ b/solution.py
@@ -1,6 +1,10 @@
+import functools
+
 import jax
 import jax.numpy as jnp
 from jax import lax
+from jax.experimental import pallas as pl
+from jax.experimental.pallas import tpu as pltpu
 from jax.sharding import PartitionSpec as P
 
 H = 8
@@ -430,6 +434,752 @@
     )
 
 
+BF = jnp.bfloat16
+F32 = jnp.float32
+RIM = 8
+NN = (((1,), (0,)), ((), ()))
+NT = (((1,), (1,)), ((), ()))
+TN = (((0,), (0,)), ((), ()))
+
+
+def dot_low(a, b, dims=NN):
+    return lax.dot_general(a, b, dims, preferred_element_type=F32)
+
+
+def parts_of(a):
+    if a.dtype == BF:
+        return (a,)
+    high = a.astype(BF)
+    return high, (a - high.astype(F32)).astype(BF)
+
+
+def mm(a, b, dims=NN):
+    a_parts, b_parts = parts_of(a), parts_of(b)
+    total = dot_low(a_parts[0], b_parts[0], dims)
+    if len(b_parts) > 1:
+        total = total + dot_low(a_parts[0], b_parts[1], dims)
+    if len(a_parts) > 1:
+        total = total + dot_low(a_parts[1], b_parts[0], dims)
+    return total
+
+
+def mm1(a, b, dims=NN):
+    return dot_low(a.astype(BF), b.astype(BF), dims)
+
+
+def begin_of(pos, starts_ref):
+    begin = jnp.zeros_like(pos)
+    for i in range(starts_ref.shape[0]):
+        begin = jnp.maximum(begin, jnp.where(pos >= starts_ref[i], starts_ref[i], 0))
+    return begin
+
+
+def begin_at(pos, starts_ref):
+    begin = jnp.int32(0)
+    for i in range(starts_ref.shape[0]):
+        begin = jnp.maximum(begin, jnp.where(starts_ref[i] <= pos, starts_ref[i], 0))
+    return begin
+
+
+def chunk_marks(n, size, starts_ref):
+    first = n * size
+    col = begin_of(first + lax.broadcasted_iota(jnp.int32, (size, 1), 0), starts_ref)
+    last = begin_at(first + size - 1, starts_ref)
+    keep = (col < first).astype(F32)
+    tail = (col == last).astype(F32)
+    whole = (last < first).astype(F32)
+    return col, keep, tail, whole
+
+
+def chunk_masks(n, size, col, starts_ref):
+    across = begin_of(n * size + lax.broadcasted_iota(jnp.int32, (1, size), 1), starts_ref)
+    here = lax.broadcasted_iota(jnp.int32, (size, size), 0)
+    there = lax.broadcasted_iota(jnp.int32, (size, size), 1)
+    same = col == across
+    return here, there, same & (here > there), same & (here >= there)
+
+
+def conv_chunk(n, size, pad, conv, col):
+    depth = n * size + lax.broadcasted_iota(jnp.int32, (size, 1), 0) - col
+    pre = conv[0:1, :] * pad[pl.ds(RIM + n * size, size), :]
+    for tap in range(1, conv.shape[0]):
+        match = (depth >= tap).astype(F32)
+        pre = pre + conv[tap : tap + 1, :] * pad[pl.ds(RIM - tap + n * size, size), :] * match
+    return pre
+
+
+def front_kernel(taps, place_ref, starts_ref, *refs):
+    n_seq = refs[-1].shape[0]
+    x_refs = refs[:n_seq]
+    (
+        got_ref,
+        act1_ref,
+        proj_ref,
+        rates_ref,
+        o_ref,
+        act2_ref,
+        inv_ref,
+        w_ref,
+        att_ref,
+        p_ref,
+        u_ref,
+        s_ref,
+        conv_ref,
+        gains_ref,
+        beta_ref,
+        head_ref,
+        pad,
+        lower,
+        tmp,
+        q_scr,
+        k_scr,
+        v_scr,
+        add,
+    ) = refs[n_seq:]
+    place = place_ref[0]
+    size = x_refs[0].shape[0]
+    dk = o_ref.shape[1]
+    half = n_seq // 2
+    z, side = place // 2, lax.rem(place, 2)
+    gains = jnp.concatenate([got_ref[s, size + 4 : size + 6, 0:dk] for s in range(n_seq)], 1).astype(F32)
+    gains_ref[...] = jnp.zeros_like(gains_ref)
+    gains_ref[0:2, :] = gains
+    beta = jnp.concatenate([got_ref[s, size + 8 : size + 16, 0:dk] for s in range(n_seq)], 1)
+    beta_ref[...] = beta
+    head_gain = got_ref[0, size + 6 : size + 7, 0:dk].astype(F32)
+    for s in range(1, n_seq):
+        head_gain = head_gain + got_ref[s, size + 6 : size + 7, 0:dk].astype(F32)
+    head_ref[...] = jnp.broadcast_to(head_gain, head_ref.shape)
+    conv_parts = []
+    for part in range(3):
+        block = part * n_seq + place
+        shard = block // 3
+        offset = pl.multiple_of((block - shard * 3) * dk, dk)
+        conv_parts.append(got_ref[shard, size : size + 8, pl.ds(offset, dk)])
+    conv = jnp.concatenate(conv_parts, 1).astype(F32)
+    conv_ref[...] = conv
+    conv = conv[0:taps]
+    weight = got_ref[:, 0:size, :].reshape(n_seq * size, 3 * dk)
+    lanes = lax.broadcasted_iota(jnp.int32, (size, 8), 1)
+    pad[0:RIM, :] = jnp.zeros((RIM, 3 * dk), F32)
+    for k in range(half):
+        for j in range(2):
+            chunk = lax.rem(z - k + half, half) * 2 + (side if j == 0 else 1 - side)
+            at = pl.multiple_of(chunk * size, size)
+            rows = x_refs[2 * k + j][...].astype(F32)
+            inv = lax.rsqrt(jnp.mean(rows * rows, -1, keepdims=True) + EPS_NORM)
+            act = ((rows * inv) * gains[0:1]).astype(BF)
+            act1_ref[pl.ds(at, size), :] = act
+            proj = dot_low(act, weight).astype(BF)
+            proj_ref[pl.ds(at, size), :] = proj
+            pad[pl.ds(pl.multiple_of(RIM + at, 8), size), :] = proj.astype(F32)
+            logits = dot_low(act, beta, NT)
+            rate = jax.nn.sigmoid(jnp.sum(jnp.where(lanes == place, logits, 0.0), 1, keepdims=True))
+            rates_ref[pl.ds(at, size), :] = jnp.broadcast_to(rate, (size, dk))
+    marks = []
+    for n in range(n_seq):
+        at = n * size
+        col, keep, tail, whole = chunk_marks(n, size, starts_ref)
+        marks.append((keep, tail, whole))
+        pre = conv_chunk(n, size, pad, conv, col)
+        act = pre * jax.nn.sigmoid(pre)
+        q_raw, k_raw, v_raw = act[:, :dk], act[:, dk : 2 * dk], act[:, 2 * dk :]
+        q = (q_raw * lax.rsqrt(jnp.sum(q_raw * q_raw, -1, keepdims=True) + EPS_UNIT)).astype(BF)
+        key = (k_raw * lax.rsqrt(jnp.sum(k_raw * k_raw, -1, keepdims=True) + EPS_UNIT)).astype(BF)
+        q_scr[pl.ds(at, size), :] = q
+        k_scr[pl.ds(at, size), :] = key
+        v_scr[pl.ds(at, size), :] = v_raw.astype(BF)
+        here, there, strict, incl = chunk_masks(n, size, col, starts_ref)
+        rate = rates_ref[pl.ds(at, size), :]
+        low = jnp.where(strict, dot_low(key, key, NT) * rate, 0.0)
+        att_ref[n] = jnp.where(incl, dot_low(q, key, NT) * (dk**-0.5), 0.0)
+        lower[n] = low
+        eye = (here == there).astype(F32)
+        inv_ref[n] = eye - jnp.where((here // 2) == (there // 2), low, 0.0)
+    span = 2
+    while span < size:
+        here = lax.broadcasted_iota(jnp.int32, (size, size), 0)
+        there = lax.broadcasted_iota(jnp.int32, (size, size), 1)
+        cross = ((here // (2 * span)) == (there // (2 * span))) & ((here // span) != (there // span))
+        for n in range(n_seq):
+            tmp[n] = mm(inv_ref[n], jnp.where(cross, lower[n], 0.0))
+        for n in range(n_seq):
+            inv_ref[n] = inv_ref[n] - mm(tmp[n], inv_ref[n])
+        span *= 2
+    for n in range(n_seq):
+        keep, tail, whole = marks[n]
+        rows = pl.ds(n * size, size)
+        rate = rates_ref[rows, :]
+        key = k_scr[rows, :]
+        inv = inv_ref[n]
+        w = mm(inv, rate * key.astype(F32))
+        base = mm(inv, rate * v_scr[rows, :].astype(F32))
+        w_ref[n] = w
+        u_ref[n] = base
+        p_ref[n] = mm(key, (tail * keep) * w, TN)
+        add[n] = mm(key, tail * base, TN)
+    state = jnp.zeros((dk, dk), F32)
+    for n in range(n_seq):
+        s_ref[n] = state
+        if n + 1 < n_seq:
+            state = marks[n][2] * state - mm(p_ref[n], state) + add[n]
+    for n in range(n_seq):
+        keep, tail, whole = marks[n]
+        rows = pl.ds(n * size, size)
+        state = s_ref[n]
+        u = u_ref[n] - keep * mm(w_ref[n], state)
+        u_ref[n] = u
+        out = (keep * (dk**-0.5)) * mm(q_scr[rows, :], state) + mm(att_ref[n], u)
+        o_ref[rows, :] = out
+        inv = lax.rsqrt(jnp.mean(out * out, -1, keepdims=True) + EPS_HEAD)
+        act2_ref[n] = ((out * inv) * head_gain).astype(BF)
+
+
+def back_kernel(taps, starts_ref, *refs):
+    (
+        dact_ref,
+        o_ref,
+        head_ref,
+        conv_ref,
+        proj_ref,
+        rates_ref,
+        inv_ref,
+        w_ref,
+        att_ref,
+        p_ref,
+        u_ref,
+        s_ref,
+        dproj_ref,
+        dlog_ref,
+        gconv_ref,
+        ghead_ref,
+        pad,
+        pre_scr,
+        dpre,
+        do_scr,
+        g_scr,
+        add,
+        x_scr,
+        q_scr,
+        k_scr,
+    ) = refs
+    n_seq, size, dk = dact_ref.shape
+    scale = dk**-0.5
+    head_gain = head_ref[0:1, :]
+    conv = conv_ref[0:taps, :]
+    total = n_seq * size
+    pad[0:RIM, :] = jnp.zeros((RIM, 3 * dk), F32)
+    pad[pl.ds(RIM, total), :] = proj_ref[...].astype(F32)
+    dpre[pl.ds(total, RIM), :] = jnp.zeros((RIM, 3 * dk), F32)
+    marks = []
+    ghead = jnp.zeros((1, dk), F32)
+    for n in range(n_seq):
+        rows = pl.ds(n * size, size)
+        col, keep, tail, whole = chunk_marks(n, size, starts_ref)
+        marks.append((col, keep, tail, whole))
+        pre = conv_chunk(n, size, pad, conv, col)
+        pre_scr[rows, :] = pre
+        act = pre * jax.nn.sigmoid(pre)
+        q_raw, k_raw = act[:, :dk], act[:, dk : 2 * dk]
+        q = (q_raw * lax.rsqrt(jnp.sum(q_raw * q_raw, -1, keepdims=True) + EPS_UNIT)).astype(BF)
+        key = (k_raw * lax.rsqrt(jnp.sum(k_raw * k_raw, -1, keepdims=True) + EPS_UNIT)).astype(BF)
+        q_scr[rows, :] = q
+        k_scr[rows, :] = key
+        out = o_ref[rows, :]
+        inv = lax.rsqrt(jnp.mean(out * out, -1, keepdims=True) + EPS_HEAD)
+        ohat = out * inv
+        d_act2 = dact_ref[n].astype(F32)
+        ghead = ghead + jnp.sum(d_act2 * ohat, 0, keepdims=True)
+        lean = d_act2 * head_gain
+        d_out = inv * (lean - ohat * jnp.mean(lean * ohat, -1, keepdims=True))
+        do_scr[rows, :] = d_out
+        g_scr[rows, :] = mm(att_ref[n], d_out, TN)
+    ghead_ref[...] = jnp.broadcast_to(ghead, ghead_ref.shape)
+    for n in range(n_seq):
+        rows = pl.ds(n * size, size)
+        col, keep, tail, whole = marks[n]
+        add[n] = mm(q_scr[rows, :], (scale * keep) * do_scr[rows, :], TN) - mm(w_ref[n], keep * g_scr[rows, :], TN)
+    grad = jnp.zeros((dk, dk), F32)
+    for n in range(n_seq - 1, -1, -1):
+        x_scr[n] = grad
+        if n > 0:
+            grad = marks[n][3] * grad - mm(p_ref[n], grad, TN) + add[n]
+    gconv = [jnp.zeros((1, 3 * dk), F32) for _ in range(taps)]
+    for n in range(n_seq - 1, -1, -1):
+        rows = pl.ds(n * size, size)
+        col, keep, tail, whole = marks[n]
+        here, there, strict, incl = chunk_masks(n, size, col, starts_ref)
+        rate = rates_ref[rows, :]
+        key, q = k_scr[rows, :], q_scr[rows, :]
+        key_f, q_f = key.astype(F32), q.astype(F32)
+        pre = pre_scr[rows, :]
+        sig = jax.nn.sigmoid(pre)
+        act = pre * sig
+        value = act[:, 2 * dk :].astype(BF).astype(F32)
+        grad, state, u = x_scr[n], s_ref[n], u_ref[n]
+        d_out = do_scr[rows, :]
+        d_u = g_scr[rows, :] + tail * mm(key, grad)
+        d_r = mm(inv_ref[n], d_u, TN)
+        d_att = jnp.where(incl, mm(d_out, u, NT), 0.0)
+        d_low = jnp.where(strict, -mm(d_r, u, NT), 0.0)
+        d_q = keep * mm(d_out, state, NT) + mm(d_att, key)
+        d_kb = mm(d_low, key) - keep * mm(d_r, state, NT)
+        d_k = (
+            scale * mm(d_att, q, TN)
+            + mm(d_low, rate * key_f, TN)
+            + tail * mm(u, grad, NT)
+            + rate * d_kb
+        )
+        d_v = rate * d_r
+        d_rate = jnp.sum(d_r * value + d_kb * key_f, -1, keepdims=True)
+        d_q = d_q * scale
+        q_raw, k_raw = act[:, :dk], act[:, dk : 2 * dk]
+        q_inv = lax.rsqrt(jnp.sum(q_raw * q_raw, -1, keepdims=True) + EPS_UNIT)
+        k_inv = lax.rsqrt(jnp.sum(k_raw * k_raw, -1, keepdims=True) + EPS_UNIT)
+        q_unit, k_unit = q_raw * q_inv, k_raw * k_inv
+        d_q = q_inv * (d_q - q_unit * jnp.sum(d_q * q_unit, -1, keepdims=True))
+        d_k = k_inv * (d_k - k_unit * jnp.sum(d_k * k_unit, -1, keepdims=True))
+        d_act = jnp.concatenate([d_q, d_k, d_v], 1)
+        d_pre = d_act * sig * (1.0 + pre * (1.0 - sig))
+        dpre[rows, :] = d_pre
+        pos = n * size + lax.broadcasted_iota(jnp.int32, (size, 1), 0)
+        d_proj = conv[0:1, :] * d_pre
+        gconv[0] = gconv[0] + jnp.sum(d_pre * pad[pl.ds(RIM + n * size, size), :], 0, keepdims=True)
+        for tap in range(1, taps):
+            later = pos + tap
+            match = ((begin_of(later, starts_ref) <= pos) & (later < total)).astype(F32)
+            d_proj = d_proj + conv[tap : tap + 1, :] * dpre[pl.ds(n * size + tap, size), :] * match
+            reach = (pos - col >= tap).astype(F32)
+            gconv[tap] = gconv[tap] + jnp.sum(
+                d_pre * reach * pad[pl.ds(RIM - tap + n * size, size), :], 0, keepdims=True
+            )
+        dproj_ref[n, 0:size, :] = d_proj.astype(BF)
+        one_rate = rate[:, 0:1]
+        d_logit = d_rate * one_rate * (1.0 - one_rate)
+        spread = jnp.broadcast_to(d_logit, (size, dk)).T
+        row_form = jnp.concatenate([spread[0:16], jnp.zeros((16, 2 * dk), F32)], 1).astype(BF)
+        dproj_ref[n, pl.ds(size, 16), :] = row_form
+        dlog_ref[pl.ds(n, 1), :] = spread[0:1]
+    gconv_ref[...] = jnp.zeros_like(gconv_ref)
+    for tap in range(taps):
+        gconv_ref[tap : tap + 1, :] = gconv[tap]
+
+
+def mid_kernel(act2_ref, weight_ref, x_ref, gains_ref, resid_ref, act3_ref):
+    heads = act2_ref.shape[0]
+    act2 = jnp.concatenate([act2_ref[h] for h in range(heads)], 1)
+    resid = x_ref[...].astype(F32) + dot_low(act2, weight_ref[...])
+    resid_ref[...] = resid
+    inv = lax.rsqrt(jnp.mean(resid * resid, -1, keepdims=True) + EPS_NORM)
+    act3_ref[...] = ((resid * inv) * gains_ref[1:2, :]).astype(BF)
+
+
+def feed_kernel(act3_ref, cot_ref, gu_ref, down_ref, part_ref, act4_ref, dgu_ref, down):
+    hidden, wide = down_ref.shape[0], down.shape[0]
+    down[0:hidden, :] = down_ref[...]
+    if wide > hidden:
+        down[hidden:wide, :] = jnp.zeros((wide - hidden, down.shape[1]), BF)
+    gate_up = dot_low(act3_ref[...], gu_ref[...])
+    gate, up = gate_up[:, :wide], gate_up[:, wide:]
+    sig = jax.nn.sigmoid(gate)
+    silu = gate * sig
+    act4_ref[...] = (silu * up).astype(BF)
+    d_act4 = dot_low(cot_ref[...], down[...], NT)
+    d_gate = d_act4 * up * sig * (1.0 + gate * (1.0 - sig))
+    d_gu = jnp.concatenate([d_gate, d_act4 * silu], 1).astype(BF)
+    dgu_ref[...] = d_gu
+    part_ref[...] = dot_low(d_gu, gu_ref[...], NT).astype(BF)
+
+
+def turn_kernel(heads, dact3_ref, resid_ref, cot_ref, gains_ref, weight_ref, dresid_ref, low_ref, dact2_ref):
+    resid = resid_ref[...]
+    inv = lax.rsqrt(jnp.mean(resid * resid, -1, keepdims=True) + EPS_NORM)
+    rhat = resid * inv
+    lean = dact3_ref[...] * gains_ref[1:2, :]
+    d_resid = cot_ref[...].astype(F32) + inv * (lean - rhat * jnp.mean(lean * rhat, -1, keepdims=True))
+    dresid_ref[...] = d_resid
+    low = d_resid.astype(BF)
+    low_ref[...] = low
+    d_act2 = dot_low(low, weight_ref[...], NT).astype(BF)
+    dk = d_act2.shape[1] // heads
+    for h in range(heads):
+        dact2_ref[h] = d_act2[:, h * dk : (h + 1) * dk]
+
+
+def last_kernel(got_ref, weight_ref, beta_ref, x_ref, gains_ref, dresid_ref, out_ref):
+    heads = got_ref.shape[0]
+    size = x_ref.shape[0]
+    dk = got_ref.shape[2] // 3
+    d_proj = jnp.concatenate(
+        [got_ref[h, 0:size, part * dk : (part + 1) * dk] for part in range(3) for h in range(heads)], 1
+    )
+    d_logits = jnp.concatenate([got_ref[h, size : size + 1, 0:dk] for h in range(heads)], 0)
+    d_act1 = dot_low(d_proj, weight_ref[...], NT) + dot_low(d_logits, beta_ref[0:heads, :], TN)
+    rows = x_ref[...].astype(F32)
+    inv = lax.rsqrt(jnp.mean(rows * rows, -1, keepdims=True) + EPS_NORM)
+    xhat = rows * inv
+    lean = d_act1 * gains_ref[0:1, :]
+    out = dresid_ref[...] + inv * (lean - xhat * jnp.mean(lean * xhat, -1, keepdims=True))
+    out_ref[...] = out.astype(BF)
+
+
+def local_call(kernel, outs, args, scratch=(), smem=0, flops=0, name=None):
+    space = [pl.BlockSpec(memory_space=pltpu.SMEM)] * smem
+    space += [pl.BlockSpec(memory_space=pltpu.VMEM)] * (len(args) - smem)
+    moved = sum(a.size * a.dtype.itemsize for a in args) + sum(o.size * o.dtype.itemsize for o in outs)
+    return pl.pallas_call(
+        kernel,
+        out_shape=tuple(outs),
+        in_specs=space,
+        out_specs=tuple(pl.BlockSpec(memory_space=pltpu.VMEM) for _ in outs),
+        scratch_shapes=list(scratch),
+        compiler_params=pltpu.CompilerParams(vmem_limit_bytes=56 * 2**20),
+        cost_estimate=pl.CostEstimate(flops=flops, bytes_accessed=moved, transcendentals=0),
+        name=name,
+    )(*args)
+
+
+def head_plan(
+    block_input,
+    cotangent,
+    doc_starts,
+    qkv_weight,
+    beta_weight,
+    conv_weight,
+    norm_gains,
+    head_gain,
+    out_weight,
+    gate_up_weight,
+    down_weight,
+):
+    x, cot = block_input[0], cotangent[0]
+    starts = doc_starts[0]
+    size, width = x.shape
+    n_seq, n_row = lax.axis_size("seq"), lax.axis_size("row")
+    place, row = lax.axis_index("seq"), lax.axis_index("row")
+    half = n_seq // 2
+    z, side = place // 2, place % 2
+    total = n_seq * size
+    taps = conv_weight.shape[0]
+    hidden = down_weight.shape[0]
+    wide = -(-hidden // 128) * 128
+    shape = jax.ShapeDtypeStruct
+
+    def flip(v):
+        return lax.ppermute(v, "seq", [(s, s ^ 1) for s in range(n_seq)])
+
+    def roll(v, k):
+        return lax.ppermute(v, "seq", [(s, (s // 2 + k) % half * 2 + s % 2) for s in range(n_seq)])
+
+    def core(v):
+        return lax.ppermute(v, "row", [(r, r ^ 1) for r in range(n_row)])
+
+    def across(v):
+        return lax.ppermute(v, "row", [(r, r ^ 2) for r in range(n_row)])
+
+    pairs = [
+        (s * n_row + r, (r * 2 + s // n_row) * n_row + s % n_row)
+        for s in range(n_seq)
+        for r in range(n_row)
+    ]
+
+    def spread(v):
+        return lax.ppermute(v, ("seq", "row"), pairs)
+
+    def collect(v):
+        return lax.ppermute(v, ("seq", "row"), [(b, a) for a, b in pairs])
+
+    def group_gather(v):
+        y, s = across(v), flip(v)
+        four = jnp.stack([v, y, s, flip(y)])
+        return jnp.concatenate([four, core(four)], 0).reshape(8 * v.shape[0], v.shape[1])
+
+    def group_sum(parts):
+        mine = parts[0:4].astype(F32) + core(parts[4:8]).astype(F32)
+        low = mine.astype(BF)
+        first = mine[1] + flip(low[3]).astype(F32)
+        second = mine[0] + flip(low[2]).astype(F32)
+        return second + across(first.astype(BF)).astype(F32)
+
+    def row_pieces(v):
+        return [lax.dynamic_index_in_dim(v, row ^ m, v.ndim - 3, False) for m in range(n_row)]
+
+    def row_sum(pieces):
+        got = core(jnp.stack([pieces[1], pieces[3]])).astype(F32)
+        first = pieces[0].astype(F32) + got[0]
+        second = pieces[2].astype(F32) + got[1]
+        return first + across(second.astype(BF)).astype(F32)
+
+    def row_gather(v):
+        pair = jnp.stack([v, core(v)])
+        four = jnp.concatenate([pair, across(pair)], 0)
+        return [lax.dynamic_index_in_dim(four, row ^ m, 0, False) for m in range(n_row)]
+
+    near = flip(x)
+    pieces = [x, near]
+    for k in range(1, half):
+        far = roll(x, k)
+        pieces += [far, flip(far)]
+    by_head = qkv_weight.reshape(size, 3, n_seq, width // n_seq).transpose(2, 0, 1, 3)
+    by_head = by_head.reshape(n_seq, size, 3 * width // n_seq)
+    cols = by_head.shape[2]
+    lane = jnp.arange(128)
+    per = head_gain.shape[0]
+    head_row = jnp.where(lane // per == place, jnp.tile(head_gain, 128 // per), jnp.zeros((), BF))
+
+    def wide_rows(v):
+        return jnp.pad(v, ((0, 0), (0, cols - v.shape[1])))
+
+    small = jnp.concatenate(
+        [
+            conv_weight,
+            wide_rows(norm_gains),
+            wide_rows(head_row[None]),
+            jnp.zeros((1, cols), BF),
+            wide_rows(beta_weight.T),
+        ],
+        0,
+    )
+    payload = jnp.concatenate([by_head, jnp.broadcast_to(small[None], (n_seq,) + small.shape)], 1)
+    got = lax.all_to_all(payload, "seq", 0, 0)
+
+    def columns(block):
+        gate = lax.dynamic_slice_in_dim(gate_up_weight, block * hidden, hidden, 1)
+        up = lax.dynamic_slice_in_dim(gate_up_weight, (n_seq + block) * hidden, hidden, 1)
+        gap = jnp.zeros((size, wide - hidden), BF)
+        return jnp.concatenate([gate, gap, up, gap], 1)
+
+    own_cols = columns(side * n_row + row)
+    other_cols = flip(columns((1 - side) * n_row + row))
+    pair_cols = jnp.where(
+        side == 0, jnp.stack([own_cols, other_cols]), jnp.stack([other_cols, own_cols])
+    ).reshape(2 * size, 2 * wide)
+    w_gu = jnp.zeros((half, 2 * size, 2 * wide), BF)
+    w_gu = lax.dynamic_update_index_in_dim(w_gu, pair_cols, z, 0)
+    for k in range(1, half):
+        w_gu = lax.dynamic_update_index_in_dim(w_gu, roll(pair_cols, k), (z - k) % half, 0)
+    w_gu = w_gu.reshape(total, 2 * wide)
+    w_down = spread(down_weight)
+    cot_all = group_gather(cot)
+    w_out = lax.all_gather(out_weight, "seq", axis=0, tiled=True)
+    w_qkv = lax.all_gather(qkv_weight, "seq", axis=0, tiled=True)
+
+    dk = width // n_seq
+    square = shape((n_seq, size, dk), F32)
+    (
+        act1,
+        proj,
+        rates,
+        outs,
+        act2,
+        inverse,
+        w_mat,
+        att,
+        p_mat,
+        u_mat,
+        states,
+        conv,
+        gains,
+        beta,
+        head,
+    ) = local_call(
+        functools.partial(front_kernel, taps),
+        [
+            shape((total, width), BF),
+            shape((total, 3 * dk), BF),
+            shape((total, dk), F32),
+            shape((total, dk), F32),
+            shape((n_seq, size, dk), BF),
+            square,
+            square,
+            square,
+            square,
+            square,
+            square,
+            shape((8, 3 * dk), F32),
+            shape((8, width), F32),
+            shape((8, width), BF),
+            shape((8, dk), F32),
+        ],
+        [place.reshape(1), starts, *pieces, got],
+        scratch=[
+            pltpu.VMEM((RIM + total, 3 * dk), F32),
+            pltpu.VMEM((n_seq, size, size), F32),
+            pltpu.VMEM((n_seq, size, size), F32),
+            pltpu.VMEM((total, dk), BF),
+            pltpu.VMEM((total, dk), BF),
+            pltpu.VMEM((total, dk), BF),
+            pltpu.VMEM((n_seq, dk, dk), F32),
+        ],
+        smem=2,
+        flops=2 * 10**10,
+        name="front",
+    )
+    act2 = lax.all_to_all(act2, "seq", 0, 0)
+    resid, act3 = local_call(
+        mid_kernel,
+        [shape((size, width), F32), shape((size, width), BF)],
+        [act2, w_out, x, gains],
+        flops=2 * size * width * width,
+        name="mid",
+    )
+    act3_all = group_gather(act3)
+    block = total // 4
+    wide_block = pl.BlockSpec((block, width), lambda i: (i, 0))
+    d_parts, act4, d_gu = pl.pallas_call(
+        feed_kernel,
+        grid=(4,),
+        out_shape=(
+            shape((total, width), BF),
+            shape((total, wide), BF),
+            shape((total, 2 * wide), BF),
+        ),
+        in_specs=[
+            wide_block,
+            wide_block,
+            pl.BlockSpec((width, 2 * wide), lambda i: (0, 0)),
+            pl.BlockSpec((hidden, width), lambda i: (0, 0)),
+        ],
+        out_specs=(
+            wide_block,
+            pl.BlockSpec((block, wide), lambda i: (i, 0)),
+            pl.BlockSpec((block, 2 * wide), lambda i: (i, 0)),
+        ),
+        scratch_shapes=[pltpu.VMEM((wide, width), BF)],
+        compiler_params=pltpu.CompilerParams(vmem_limit_bytes=56 * 2**20),
+        cost_estimate=pl.CostEstimate(
+            flops=10 * total * width * wide, bytes_accessed=14 * 2**20, transcendentals=0
+        ),
+        name="feed",
+    )(act3_all, cot_all, w_gu, w_down)
+    d_act3 = group_sum(d_parts.reshape(8, size, width))
+    mixed_parts = jnp.dot(act4[:, :hidden], w_down, preferred_element_type=F32).astype(BF)
+    mixed = (resid + group_sum(mixed_parts.reshape(8, size, width))).astype(BF)
+    grad_down = tok_dot(act4, cot_all)[:hidden].astype(BF)
+    grad_gu = tok_dot(act3_all, d_gu).astype(BF)
+    d_resid, d_low, d_act2 = local_call(
+        functools.partial(turn_kernel, n_seq),
+        [shape((size, width), F32), shape((size, width), BF), shape((n_seq, size, dk), BF)],
+        [d_act3, resid, cot, gains, w_out],
+        flops=2 * size * width * width,
+        name="turn",
+    )
+    d_act2 = lax.all_to_all(d_act2, "seq", 0, 0)
+    d_proj, d_log, g_conv, g_head = local_call(
+        functools.partial(back_kernel, taps),
+        [
+            shape((n_seq, size + 16, 3 * dk), BF),
+            shape((n_seq, size), F32),
+            shape((8, 3 * dk), F32),
+            shape((8, dk), F32),
+        ],
+        [starts, d_act2, outs, head, conv, proj, rates, inverse, w_mat, att, p_mat, u_mat, states],
+        scratch=[
+            pltpu.VMEM((RIM + total, 3 * dk), F32),
+            pltpu.VMEM((total, 3 * dk), F32),
+            pltpu.VMEM((RIM + total, 3 * dk), F32),
+            pltpu.VMEM((total, dk), F32),
+            pltpu.VMEM((total, dk), F32),
+            pltpu.VMEM((n_seq, dk, dk), F32),
+            pltpu.VMEM((n_seq, dk, dk), F32),
+            pltpu.VMEM((total, dk), BF),
+            pltpu.VMEM((total, dk), BF),
+        ],
+        smem=1,
+        flops=2 * 10**10,
+        name="back",
+    )
+    back = lax.all_to_all(d_proj, "seq", 0, 0)
+    (input_gradient,) = local_call(
+        last_kernel,
+        [shape((size, width), BF)],
+        [back, w_qkv, beta, x, gains, d_resid],
+        flops=6 * size * width * width,
+        name="last",
+    )
+
+    own = side
+    blocks = grad_gu.reshape(half, 2 * size, 2 * wide)
+    gu_sum = lax.dynamic_index_in_dim(blocks, z, 0, False).astype(F32)
+    for k in range(1, half):
+        gu_sum = gu_sum + roll(
+            lax.dynamic_index_in_dim(blocks, (z + k) % half, 0, False), k
+        ).astype(F32)
+    gu_sum = gu_sum.astype(BF).reshape(2, size, 2 * wide)
+    gu_mine = lax.dynamic_index_in_dim(gu_sum, side, 0, False)
+    gu_other = flip(lax.dynamic_index_in_dim(gu_sum, 1 - side, 0, False))
+    gu_two = jnp.where(side == 0, jnp.stack([gu_mine, gu_other]), jnp.stack([gu_other, gu_mine]))
+    gu_rows = row_gather(gu_two)
+    gu_blocks = [gu_rows[b % n_row][b // n_row] for b in range(n_seq)]
+    red_gu = jnp.concatenate(
+        [b[:, :hidden] for b in gu_blocks] + [b[:, wide : wide + hidden] for b in gu_blocks], 1
+    ).astype(F32)
+    down_here = collect(grad_down).reshape(n_row, hidden // n_row, width)
+    red_down = jnp.concatenate(row_gather(row_sum(row_pieces(down_here)).astype(BF)), 0).astype(F32)
+
+    def seq_row_sum(full):
+        cols = full.shape[1]
+        cut = full.reshape(n_seq, n_row, size // n_row, cols)
+        mine = row_sum(row_pieces(cut)).astype(BF)
+        return lax.all_to_all(mine, "seq", 0, 0)
+
+    act2_rows = act2.transpose(1, 0, 2).reshape(size, width)
+    grad_out = tok_dot(act2_rows, d_low).astype(BF)
+    out_piece = seq_row_sum(grad_out).astype(F32).sum(0).astype(BF)
+    red_out = jnp.concatenate(row_gather(out_piece), 0).astype(F32)
+    grad_qkv = tok_dot(act1, d_proj[:, :size].reshape(total, 3 * dk)).astype(BF)
+    qkv_piece = seq_row_sum(grad_qkv)
+    qkv_piece = qkv_piece.reshape(n_seq, size // n_row, 3, dk).transpose(1, 2, 0, 3)
+    qkv_piece = qkv_piece.reshape(size // n_row, 3 * width)
+    red_qkv = jnp.concatenate(row_gather(qkv_piece), 0).astype(F32)
+    g_beta = jnp.dot(
+        d_log.astype(BF).reshape(1, total), act1, preferred_element_type=F32
+    ).reshape(n_seq, 1, size)
+    g_conv_rows = g_conv[:taps].reshape(taps * 3, dk)
+    small_out = jnp.concatenate(
+        [
+            g_beta,
+            jnp.broadcast_to(g_conv_rows[None], (n_seq, taps * 3, dk)),
+            jnp.broadcast_to(g_head[None, 0:1], (n_seq, 1, dk)),
+            jnp.zeros((n_seq, 2, dk), F32),
+        ],
+        1,
+    )
+    small_in = lax.all_to_all(small_out, "seq", 0, 0)
+    small_in = small_in + core(small_in)
+    small_in = small_in + across(small_in)
+    red_beta = small_in[:, 0, :].T
+    conv_in = small_in[:, 1 : 1 + taps * 3].reshape(n_seq, taps, 3, dk)
+    conv_in = conv_in.transpose(1, 2, 0, 3).reshape(taps, 3 * width)
+    red_conv = lax.dynamic_slice_in_dim(conv_in, place * 3 * dk, 3 * dk, 1)
+    red_head = lax.dynamic_slice_in_dim(small_in[:, 1 + taps * 3].sum(0), place * per, per, 0)
+    own_gains = norm_gains.astype(F32)
+    first_gain = (
+        jnp.sum(qkv_weight.astype(F32) * red_qkv, 1) + jnp.sum(beta_weight.astype(F32) * red_beta, 1)
+    ) / own_gains[0]
+    second_gain = jnp.sum(gate_up_weight.astype(F32) * red_gu, 1) / own_gains[1]
+    red_gains = jnp.stack([first_gain, second_gain])
+    return (
+        mixed[None],
+        input_gradient[None],
+        red_qkv,
+        red_beta,
+        red_conv,
+        red_gains,
+        red_head,
+        red_out,
+        red_gu,
+        red_down,
+    )
+
+
+def plan(block_input, *rest):
+    seq, row = lax.axis_size("seq"), lax.axis_size("row")
+    if seq == H and row * 2 == H and block_input.shape[1] == DK:
+        return head_plan(block_input, *rest)
+    return on_device(block_input, *rest)
+
+
 def solution(mesh):
     in_specs = (
         P("row", "seq", None),
@@ -457,5 +1207,5 @@
         P("seq", None),
     )
     return jax.shard_map(
-        on_device, mesh=mesh, in_specs=in_specs, out_specs=out_specs, check_vma=False
-    )
+        plan, mesh=mesh, in_specs=in_specs, out_specs=out_specs, check_vma=False
+    )

time: 1440 us -> 519 us (0.36)
  waiting for transfers between devices: 1000 us -> 217 us
  starting transfers between devices: 4.57 us -> 153 us
  matrix products: 157 us -> 10.8 us
  blocking collectives: 126 us -> 0 us
  Pallas kernels: 0 us -> 53 us
  local copies, waits for them, and re-layouts: 64.9 us -> 30 us
  other arithmetic: 59.5 us -> 34.1 us
    reduce_scatter x4 -> x0, waiting for transfers between devices: 396 us -> none  [the longest x1 195 us: on_device(): lax.psum_scatter(grad_gate_up.astype(jnp.bfloat16), 'seq', scatter_dimens...]
    all_gather x8 -> x2, waiting for transfers between devices: 372 us -> 0.01 us  [the longest x1 0.01 us: head_plan(): w_out = lax.all_gather(out_weight, 'seq', axis=0, tiled=True)]
    unnamed x19 -> x2, waiting for transfers between devices: 169 us -> 0.7 us
    dot_general x99 -> x2, matrix products: 138 us -> 2.74 us  [the longest x1 2.36 us: head_plan(): jnp.dot(act4[:, :hidden], w_down, preferred_element_type=F32).astype(BF)]
    ppermute x2 -> x49, waiting for transfers between devices: 4.78 us -> 121 us  [the longest x9 81.4 us: roll(): lax.ppermute(v, 'seq', [(s, (s // 2 + k) % half * 2 + s % 2) for s in ran...]
    ppermute x2 -> x49, starting transfers between devices: 3.93 us -> 111 us  [the longest x12 41.3 us: core(): return lax.ppermute(v, 'row', [(r, r ^ 1) for r in range(n_row)])]
    all_to_all x0 -> x7, waiting for transfers between devices: none -> 95.5 us  [the longest x1 59.5 us: head_plan(): act2 = lax.all_to_all(act2, 'seq', 0, 0)]
    all_gather x3 -> x0, blocking collectives: 80 us -> none  [the longest x1 31.1 us: on_device(): lax.all_gather(conv_weight, 'seq', axis=1, tiled=True)]
  transfers between devices with their start and end apart: 18 -> 58, of which waited for: 17 -> 17; matrix products, arithmetic and copies ran while one was open for 16% -> 14% of each run, Pallas kernels for 0% -> 9%
where the time goes in v1:
time: 519 us; the launch traced here: 514 us
  waiting for transfers between devices  217 us (42%)
  starting transfers between devices  153 us (29%)
  Pallas kernels  53 us (10%)
  other arithmetic  34.1 us (7%)
  local copies, waits for them, and re-layouts  30 us (6%)
  between operations  15.5 us (3%)
  matrix products  10.8 us (2%)
    ppermute x9, waiting for transfers between devices, roll(): lax.ppermute(v, 'seq', [(s, (s // 2 + k) % half * 2 + s % 2) for s in ran...  81.4 us
    all_to_all x1, waiting for transfers between devices, head_plan(): act2 = lax.all_to_all(act2, 'seq', 0, 0)  59.5 us
    pallas_call x5, Pallas kernels, local_call(): pl.pallas_call(kernel, out_shape=tuple(outs), in_specs=space, out_specs=t...  43.5 us
    ppermute x12, starting transfers between devices, core(): return lax.ppermute(v, 'row', [(r, r ^ 1) for r in range(n_row)])  41.3 us
    ppermute x9, starting transfers between devices, roll(): lax.ppermute(v, 'seq', [(s, (s // 2 + k) % half * 2 + s % 2) for s in ran...  38.1 us
    ppermute x12, waiting for transfers between devices, across(): return lax.ppermute(v, 'row', [(r, r ^ 2) for r in range(n_row)])  27.6 us
    all_to_all x2, waiting for transfers between devices, seq_row_sum(): return lax.all_to_all(mine, 'seq', 0, 0)  16.4 us
    ppermute x14, starting transfers between devices, flip(): return lax.ppermute(v, 'seq', [(s, s ^ 1) for s in range(n_seq)])  15.4 us
  transfers between devices with their start and end apart: 58, of which 17 were waited for; matrix products, arithmetic and copies ran while one was open for 14% of the time, Pallas kernels for 9%

profile of v1, /device:TPU:0, one launch (start us, length us, event | category | flops | bytes accessed | tf_op | source)
XLA Modules:
  0.0 513.8 jit_solution(15269722607866300296)
XLA Ops:
  13.1 7.4 %all-to-all-start = ((bf16[8,144,384]{2,1,0:T(8,128)(2,1)}), bf16[8,144,384]{2,1,0:T(8,128)(2,1)}, u32[]{:S(2)}, u32[]{:S(2)}) async-start(bf16[8,144,384]{2,1,0:T(8,128)(2,1)} %pad_maximum_fusion.4), calls=%async_computation | async-start | bytes 1769472 | tf_op jit(solution)/shard_map/all_to_all | solution.py:944
  30.0 7.5 %collective-permute-done.15 = bf16[128,768]{1,0:T(8,128)(2,1)S(1)} collective-permute-done((bf16[128,768]{1,0:T(8,128)(2,1)S(1)}, bf16[128,768]{1,0:T(8,128)(2,1)S(1)}, u32[]{:S(2)}, u32[]{:S(2)}) %collective-permute-start.15) | collective-permute-done | bytes 196640 | tf_op jit(solution)/shard_map/ppermute | solution.py:869
  39.1 14.8 %collective-permute-done.1.refs_2_ = bf16[128,1024]{1,0:T(8,128)(2,1)} collective-permute-done((bf16[128,1024]{1,0:T(8,128)(2,1)S(1)}, bf16[128,1024]{1,0:T(8,128)(2,1)}, u32[]{:S(2)}, u32[]{:S(2)}) %collective-permute-start.1) | collective-permute-done | bytes 262176 | tf_op jit(solution)/shard_map/ppermute | solution.py:872
  55.4 25.1 %collective-permute-done.3.refs_4_ = bf16[128,1024]{1,0:T(8,128)(2,1)} collective-permute-done((bf16[128,1024]{1,0:T(8,128)(2,1)S(1)}, bf16[128,1024]{1,0:T(8,128)(2,1)}, u32[]{:S(2)}, u32[]{:S(2)}) %collective-permute-start.3) | collective-permute-done | bytes 262176 | tf_op jit(solution)/shard_map/ppermute | solution.py:872
  85.4 6.8 %collective-permute-start.19 = (bf16[352,1024]{1,0:T(8,128)(2,1)}, bf16[352,1024]{1,0:T(8,128)(2,1)}, u32[]{:S(2)}, u32[]{:S(2)}) collective-permute-start(bf16[352,1024]{1,0:T(8,128)(2,1)} %param.21), channel_id=1, source_target_pairs={{0,0},{1,8},{2,16},{3,24},{4,1},{5,9},{6,17},{7,25},{8,2},{9,10},{... | collective-permute-start | bytes 2162696 | tf_op jit(solution)/shard_map/ppermute | solution.py:887
  92.3 4.7 collective-permute-start.16
  100.5 14.6 %front.1 = (bf16[1024,1024]{1,0:T(8,128)(2,1)}, bf16[1024,384]{1,0:T(8,128)(2,1)}, f32[1024,128]{1,0:T(8,128)}, f32[1024,128]{1,0:T(8,128)}, bf16[8,128,128]{2,1...) custom-call(s32[1]{0:T(128)} %bitcast.place_ref, ...), custom_call_target="tpu_custom_call" | custom-call | flops 20000000000 | bytes 10387492 | tf_op jit(solution)/shard_map/front/pallas_call | solution.py:830
  115.1 14.4 %all-to-all-start.1 = ((bf16[8,128,128]{2,1,0:T(8,128)(2,1)}), bf16[8,128,128]{2,1,0:T(8,128)(2,1)S(1)}, u32[]{:S(2)}, u32[]{:S(2)}) async-start(bf16[8,128,128]{2,1,0:T(8,128)(2,1)} %get-tuple-element.37), calls=%async_computation.1 | async-start | bytes 524288 | tf_op jit(solution)/shard_map/all_to_all | solution.py:1018
  132.7 59.5 %all-to-all-done.1.act2_ref = bf16[8,128,128]{2,1,0:T(8,128)(2,1)S(1)} async-done(((bf16[8,128,128]{2,1,0:T(8,128)(2,1)}), bf16[8,128,128]{2,1,0:T(8,128)(2,1)S(1)}, u32[]{:S(2)}, u32[]{:S(2)}) %all-to-all-start.1) | async-done | bytes 262176 | tf_op jit(solution)/shard_map/all_to_all | solution.py:1018
  196.9 21.2 %collective-permute-start.18 = (bf16[256,768]{1,0:T(8,128)(2,1)S(1)}, bf16[256,768]{1,0:T(8,128)(2,1)S(1)}, u32[]{:S(2)}, u32[]{:S(2)}) collective-permute-start(bf16[256,768]{1,0:T(8,128)(2,1)S(1)} %bitcast.295), channel_id=1, source_target_pairs={{0,24},{4,28},{8,0},{12,4},{16,8},{20,12},{24,16},{28,20},{1,25},{... | collective-permute-start | bytes 1179656 | tf_op jit(solution)/shard_map/ppermute | solution.py:872
  222.3 17.6 %collective-permute-done.18 = bf16[256,768]{1,0:T(8,128)(2,1)S(1)} collective-permute-done((bf16[256,768]{1,0:T(8,128)(2,1)S(1)}, bf16[256,768]{1,0:T(8,128)(2,1)S(1)}, u32[]{:S(2)}, u32[]{:S(2)}) %collective-permute-start.18) | collective-permute-done | bytes 393248 | tf_op jit(solution)/shard_map/ppermute | solution.py:872
  248.7 9.5 %feed.1 = (bf16[1024,1024]{1,0:T(8,128)(2,1)}, bf16[1024,384]{1,0:T(8,128)(2,1)}, bf16[1024,768]{1,0:T(8,128)(2,1)}) custom-call(bf16[1024,1024]{1,0:T(8,128)(2,1)} %bitcast.334, bf16[1024,1024]{1,0:T(8,128)(2,1)} %bitcast.276, bf16[1024,768]{1,0:T(8,128)(2,1)} %bitcast.286, bf16[352,1024]{1,0:T(8,128)(2,1)} %collective-permute-done.19.down_ref), custom_call_target="tpu_custom_call" | custom-call | flops 4026531840 | bytes 14680064 | tf_op jit(solution)/shard_map/feed/pallas_call | solution.py:1029
  269.1 7.2 %collective-permute-done.34 = bf16[256,768]{1,0:T(8,128)(2,1)S(1)} collective-permute-done((bf16[256,768]{1,0:T(8,128)(2,1)S(1)}, bf16[256,768]{1,0:T(8,128)(2,1)S(1)}, u32[]{:S(2)}, u32[]{:S(2)}) %collective-permute-start.34) | collective-permute-done | bytes 393248 | tf_op jit(solution)/shard_map/ppermute | solution.py:872
  276.2 16.8 %collective-permute-done.35 = bf16[256,768]{1,0:T(8,128)(2,1)S(1)} collective-permute-done((bf16[256,768]{1,0:T(8,128)(2,1)S(1)}, bf16[256,768]{1,0:T(8,128)(2,1)S(1)}, u32[]{:S(2)}, u32[]{:S(2)}) %collective-permute-start.35) | collective-permute-done | bytes 393248 | tf_op jit(solution)/shard_map/ppermute | solution.py:872
  300.9 36.8 %collective-permute-start.45 = (bf16[2,88,1024]{2,1,0:T(8,128)(2,1)S(1)}, bf16[2,88,1024]{2,1,0:T(8,128)(2,1)S(1)}, u32[]{:S(2)}, u32[]{:S(2)}) collective-permute-start(bf16[2,88,1024]{2,1,0:T(8,128)(2,1)S(1)} %pad_maximum_fusion.10), channel_id=1, source_target_pairs={{0,1},{1,0},{2,3},{3,2},{4,5},{5,4},{6,7},{7,6},{8,9},{9,8},{10,11... | collective-permute-start | bytes 1081352 | tf_op jit(solution)/shard_map/ppermute | solution.py:875
  346.2 16.1 %collective-permute-done.46 = bf16[88,1024]{1,0:T(8,128)(2,1)S(1)} collective-permute-done((bf16[88,1024]{1,0:T(8,128)(2,1)S(1)}, bf16[88,1024]{1,0:T(8,128)(2,1)S(1)}, u32[]{:S(2)}, u32[]{:S(2)}) %collective-permute-start.46) | collective-permute-done | bytes 180256 | tf_op jit(solution)/shard_map/ppermute | solution.py:878
  368.0 5.0 collective-permute-done.27
  396.1 15.9 %back.1 = (bf16[8,144,384]{2,1,0:T(8,128)(2,1)}, f32[8,128]{1,0:T(8,128)}, f32[8,384]{1,0:T(8,128)}, f32[8,128]{1,0:T(8,128)}) custom-call(s32[8]{0:T(128)} %bitcast.338, bf16[8,128,128]{2,1,0:T(8,128)(2,1)} %all-to-all-done.2.refs_0_, f32[1024,128]{1,0:T(8,128)} %get-tuple-element.44.refs_1_, f32[8,128]{1,0:T(8,128)} %get-tuple-element.45.refs_2_, ...), custom_call_target="tpu_custom_call" | custom-call | flops 20000000000 | bytes 6164512 | tf_op jit(solution)/shard_map/back/pallas_call | solution.py:830
  417.9 5.6 %all-to-all-start.5 = ((f32[8,16,128]{2,1,0:T(8,128)}), f32[8,16,128]{2,1,0:T(8,128)S(1)}, u32[]{:S(2)}, u32[]{:S(2)}) async-start(f32[8,16,128]{2,1,0:T(8,128)} %maximum_maximum_fusion), calls=%async_computation.5 | async-start | bytes 131072 | tf_op jit(solution)/shard_map/all_to_all | solution.py:1148
  424.6 5.8 %all-to-all-done.5 = f32[8,16,128]{2,1,0:T(8,128)S(1)} async-done(((f32[8,16,128]{2,1,0:T(8,128)}), f32[8,16,128]{2,1,0:T(8,128)S(1)}, u32[]{:S(2)}, u32[]{:S(2)}) %all-to-all-start.5) | async-done | bytes 65568 | tf_op jit(solution)/shard_map/all_to_all | solution.py:1148
  446.3 5.5 %all-to-all-done.4 = bf16[8,32,384]{2,1,0:T(8,128)(2,1)S(1)} async-done(((bf16[8,32,384]{2,1,0:T(8,128)(2,1)}), bf16[8,32,384]{2,1,0:T(8,128)(2,1)S(1)}, u32[]{:S(2)}, u32[]{:S(2)}) %all-to-all-start.4) | async-done | bytes 196640 | tf_op jit(solution)/shard_map/all_to_all | solution.py:1124
  462.5 10.9 %all-to-all-done.6 = bf16[8,32,1024]{2,1,0:T(8,128)(2,1)S(1)} async-done(((bf16[8,32,1024]{2,1,0:T(8,128)(2,1)}), bf16[8,32,1024]{2,1,0:T(8,128)(2,1)S(1)}, u32[]{:S(2)}, u32[]{:S(2)}) %all-to-all-start.6) | async-done | bytes 524320 | tf_op jit(solution)/shard_map/all_to_all | solution.py:1124
  485.7 13.8 %all-to-all-done.3.got_ref = bf16[8,144,384]{2,1,0:T(8,128)(2,1)S(1)} async-done(((bf16[8,144,384]{2,1,0:T(8,128)(2,1)}), bf16[8,144,384]{2,1,0:T(8,128)(2,1)S(1)}, u32[]{:S(2)}, u32[]{:S(2)}) %all-to-all-start.3) | async-done | bytes 884768 | tf_op jit(solution)/shard_map/all_to_all | solution.py:1092
  500.5 6.3 %last.1 = bf16[128,1024]{1,0:T(8,128)(2,1)} custom-call(bf16[8,144,384]{2,1,0:T(8,128)(2,1)} %copy-done.2, bf16[1024,3072]{1,0:T(8,128)(2,1)} %all-gather.5.cloned.1.call-done.weight_ref, bf16[8,1024]{1,0:T(8,128)(2,1)} %get-tuple-element.56.beta_ref, bf16[128,1024]{1,0:T(8,128)(2,1)} %bitcast.302, f32[8,1024]{1,0:T(8,128)} %get-tuple-element.38.gains_ref, ...), custom_call_target="tpu_custom_call" | custom-call | flops 805306368 | bytes 8273920 | tf_op jit(solution)/shard_map/last/pallas_call | solution.py:830
  (287 shorter events, 149.6 us)
Async XLA Ops:
  7.2 185.0 %all-gather.3.cloned.1.call-start = ((), (), s32[]{:S(2)}) async-start(), calls=%async_computation.7 | async-start | bytes 2359296 | tf_op jit(solution)/shard_map/all_gather | solution.py:964
  13.1 87.4 %all-to-all-start = ((bf16[8,144,384]{2,1,0:T(8,128)(2,1)}), bf16[8,144,384]{2,1,0:T(8,128)(2,1)}, u32[]{:S(2)}, u32[]{:S(2)}) async-start(bf16[8,144,384]{2,1,0:T(8,128)(2,1)} %pad_maximum_fusion.4), calls=%async_computation | async-start | bytes 1769472 | tf_op jit(solution)/shard_map/all_to_all | solution.py:944
  20.5 479.0 %all-gather.5.cloned.1.call-start = ((), (), s32[]{:S(2)}) async-start(), calls=%async_computation.8 | async-start | bytes 7077888 | tf_op jit(solution)/shard_map/all_gather | solution.py:965
  20.6 33.3 %collective-permute-start.1 = (bf16[128,1024]{1,0:T(8,128)(2,1)S(1)}, bf16[128,1024]{1,0:T(8,128)(2,1)}, u32[]{:S(2)}, u32[]{:S(2)}) collective-permute-start(bf16[128,1024]{1,0:T(8,128)(2,1)S(1)} %bitcast.303), channel_id=1, source_target_pairs={{0,8},{4,12},{8,16},{12,20},{16,24},{20,28},{24,0},{28,4},{1,9},{5... | collective-permute-start | bytes 786440 | tf_op jit(solution)/shard_map/ppermute | solution.py:872
  22.6 58.0 %collective-permute-start.3 = (bf16[128,1024]{1,0:T(8,128)(2,1)S(1)}, bf16[128,1024]{1,0:T(8,128)(2,1)}, u32[]{:S(2)}, u32[]{:S(2)}) collective-permute-start(bf16[128,1024]{1,0:T(8,128)(2,1)S(1)} %bitcast.304), channel_id=1, source_target_pairs={{0,16},{4,20},{8,24},{12,28},{16,0},{20,4},{24,8},{28,12},{1,17},{... | collective-permute-start | bytes 786440 | tf_op jit(solution)/shard_map/ppermute | solution.py:872
  24.9 57.3 %collective-permute-start.5 = (bf16[128,1024]{1,0:T(8,128)(2,1)S(1)}, bf16[128,1024]{1,0:T(8,128)(2,1)}, u32[]{:S(2)}, u32[]{:S(2)}) collective-permute-start(bf16[128,1024]{1,0:T(8,128)(2,1)S(1)} %bitcast.305), channel_id=1, source_target_pairs={{0,24},{4,28},{8,0},{12,4},{16,8},{20,12},{24,16},{28,20},{1,25},{... | collective-permute-start | bytes 786440 | tf_op jit(solution)/shard_map/ppermute | solution.py:872
  29.4 54.3 %collective-permute-start = (bf16[128,1024]{1,0:T(8,128)(2,1)S(1)}, bf16[128,1024]{1,0:T(8,128)(2,1)}, u32[]{:S(2)}, u32[]{:S(2)}) collective-permute-start(bf16[128,1024]{1,0:T(8,128)(2,1)S(1)} %bitcast.306), channel_id=1, source_target_pairs={{0,4},{4,0},{8,12},{12,8},{16,20},{20,16},{24,28},{28,24},{1,5},{5... | collective-permute-start | bytes 786440 | tf_op jit(solution)/shard_map/ppermute | solution.py:869
  37.5 47.9 %collective-permute-start.11 = (bf16[128,1024]{1,0:T(8,128)(2,1)S(1)}, bf16[128,1024]{1,0:T(8,128)(2,1)}, u32[]{:S(2)}, u32[]{:S(2)}) collective-permute-start(bf16[128,1024]{1,0:T(8,128)(2,1)S(1)} %bitcast.280), channel_id=1, source_target_pairs={{0,2},{1,3},{2,0},{3,1},{4,6},{5,7},{6,4},{7,5},{8,10},{9,11},{10,... | collective-permute-start | bytes 786440 | tf_op jit(solution)/shard_map/ppermute | solution.py:878
  53.9 38.4 %collective-permute-start.2 = (bf16[128,1024]{1,0:T(8,128)(2,1)}, bf16[128,1024]{1,0:T(8,128)(2,1)}, u32[]{:S(2)}, u32[]{:S(2)}) collective-permute-start(bf16[128,1024]{1,0:T(8,128)(2,1)} %collective-permute-done.1.refs_2_), channel_id=1, source_target_pairs={{0,4},{4,0},{8,12},{12,8},{16,20},{20,16},{24,28},{28,24},{1,5},{5... | collective-permute-start | bytes 786440 | tf_op jit(solution)/shard_map/ppermute | solution.py:869
  83.6 46.9 %collective-permute-start.12 = (bf16[128,1024]{1,0:T(8,128)(2,1)S(1)}, bf16[128,1024]{1,0:T(8,128)(2,1)S(1)}, u32[]{:S(2)}, u32[]{:S(2)}) collective-permute-start(bf16[128,1024]{1,0:T(8,128)(2,1)S(1)} %bitcast.281), channel_id=1, source_target_pairs={{0,4},{4,0},{8,12},{12,8},{16,20},{20,16},{24,28},{28,24},{1,5},{5... | collective-permute-start | bytes 786440 | tf_op jit(solution)/shard_map/ppermute | solution.py:869
  85.4 162.0 %collective-permute-start.19 = (bf16[352,1024]{1,0:T(8,128)(2,1)}, bf16[352,1024]{1,0:T(8,128)(2,1)}, u32[]{:S(2)}, u32[]{:S(2)}) collective-permute-start(bf16[352,1024]{1,0:T(8,128)(2,1)} %param.21), channel_id=1, source_target_pairs={{0,0},{1,8},{2,16},{3,24},{4,1},{5,9},{6,17},{7,25},{8,2},{9,10},{... | collective-permute-start | bytes 2162696 | tf_op jit(solution)/shard_map/ppermute | solution.py:887
  92.3 104.6 %collective-permute-start.16 = (bf16[256,768]{1,0:T(8,128)(2,1)S(1)}, bf16[256,768]{1,0:T(8,128)(2,1)}, u32[]{:S(2)}, u32[]{:S(2)}) collective-permute-start(bf16[256,768]{1,0:T(8,128)(2,1)S(1)} %bitcast.293), channel_id=1, source_target_pairs={{0,8},{4,12},{8,16},{12,20},{16,24},{20,28},{24,0},{28,4},{1,9},{5... | collective-permute-start | bytes 1179656 | tf_op jit(solution)/shard_map/ppermute | solution.py:872
  97.0 122.2 %collective-permute-start.17 = (bf16[256,768]{1,0:T(8,128)(2,1)S(1)}, bf16[256,768]{1,0:T(8,128)(2,1)}, u32[]{:S(2)}, u32[]{:S(2)}) collective-permute-start(bf16[256,768]{1,0:T(8,128)(2,1)S(1)} %bitcast.294), channel_id=1, source_target_pairs={{0,16},{4,20},{8,24},{12,28},{16,0},{20,4},{24,8},{28,12},{1,17},{... | collective-permute-start | bytes 1179656 | tf_op jit(solution)/shard_map/ppermute | solution.py:872
  115.1 77.1 %all-to-all-start.1 = ((bf16[8,128,128]{2,1,0:T(8,128)(2,1)}), bf16[8,128,128]{2,1,0:T(8,128)(2,1)S(1)}, u32[]{:S(2)}, u32[]{:S(2)}) async-start(bf16[8,128,128]{2,1,0:T(8,128)(2,1)} %get-tuple-element.37), calls=%async_computation.1 | async-start | bytes 524288 | tf_op jit(solution)/shard_map/all_to_all | solution.py:1018
  132.7 110.6 %collective-permute-start.14 = (bf16[4,128,1024]{2,1,0:T(8,128)(2,1)}, bf16[4,128,1024]{2,1,0:T(8,128)(2,1)}, u32[]{:S(2)}, u32[]{:S(2)}) collective-permute-start(bf16[4,128,1024]{2,1,0:T(8,128)(2,1)} %pad_maximum_fusion.2), channel_id=1, source_target_pairs={{0,1},{1,0},{2,3},{3,2},{4,5},{5,4},{6,7},{7,6},{8,9},{9,8},{10,11... | collective-permute-start | bytes 3145736 | tf_op jit(solution)/shard_map/ppermute | solution.py:875
  196.9 42.9 %collective-permute-start.18 = (bf16[256,768]{1,0:T(8,128)(2,1)S(1)}, bf16[256,768]{1,0:T(8,128)(2,1)S(1)}, u32[]{:S(2)}, u32[]{:S(2)}) collective-permute-start(bf16[256,768]{1,0:T(8,128)(2,1)S(1)} %bitcast.295), channel_id=1, source_target_pairs={{0,24},{4,28},{8,0},{12,4},{16,8},{20,12},{24,16},{28,20},{1,25},{... | collective-permute-start | bytes 1179656 | tf_op jit(solution)/shard_map/ppermute | solution.py:872
  267.2 33.6 %collective-permute-start.44 = (bf16[352,1024]{1,0:T(8,128)(2,1)S(1)}, bf16[352,1024]{1,0:T(8,128)(2,1)S(1)}, u32[]{:S(2)}, u32[]{:S(2)}) collective-permute-start(bf16[352,1024]{1,0:T(8,128)(2,1)S(1)} %slice.337), channel_id=1, source_target_pairs={{0,0},{8,1},{16,2},{24,3},{1,4},{9,5},{17,6},{25,7},{2,8},{10,9},{... | collective-permute-start | bytes 2162696 | tf_op jit(solution)/shard_map/ppermute | solution.py:890
  268.1 70.6 %collective-permute-start.24 = (bf16[4,128,1024]{2,1,0:T(8,128)(2,1)S(1)}, bf16[4,128,1024]{2,1,0:T(8,128)(2,1)S(1)}, u32[]{:S(2)}, u32[]{:S(2)}) collective-permute-start(bf16[4,128,1024]{2,1,0:T(8,128)(2,1)S(1)} %bitcast.298), channel_id=1, source_target_pairs={{0,1},{1,0},{2,3},{3,2},{4,5},{5,4},{6,7},{7,6},{8,9},{9,8},{10,11... | collective-permute-start | bytes 3145736 | tf_op jit(solution)/shard_map/ppermute | solution.py:875
  300.0 37.7 %collective-permute-start.38 = (bf16[2,128,768]{2,1,0:T(8,128)(2,1)S(1)}, bf16[2,128,768]{2,1,0:T(8,128)(2,1)S(1)}, u32[]{:S(2)}, u32[]{:S(2)}) collective-permute-start(bf16[2,128,768]{2,1,0:T(8,128)(2,1)S(1)} %maximum_select_fusion.2), channel_id=1, source_target_pairs={{0,1},{1,0},{2,3},{3,2},{4,5},{5,4},{6,7},{7,6},{8,9},{9,8},{10,11... | collective-permute-start | bytes 1179656 | tf_op jit(solution)/shard_map/ppermute | solution.py:875
  300.2 41.1 %collective-permute-start.20 = (bf16[4,128,1024]{2,1,0:T(8,128)(2,1)S(1)}, bf16[4,128,1024]{2,1,0:T(8,128)(2,1)S(1)}, u32[]{:S(2)}, u32[]{:S(2)}) collective-permute-start(bf16[4,128,1024]{2,1,0:T(8,128)(2,1)S(1)} %bitcast.299), channel_id=1, source_target_pairs={{0,1},{1,0},{2,3},{3,2},{4,5},{5,4},{6,7},{7,6},{8,9},{9,8},{10,11... | collective-permute-start | bytes 3145736 | tf_op jit(solution)/shard_map/ppermute | solution.py:875
  300.9 40.9 %collective-permute-start.45 = (bf16[2,88,1024]{2,1,0:T(8,128)(2,1)S(1)}, bf16[2,88,1024]{2,1,0:T(8,128)(2,1)S(1)}, u32[]{:S(2)}, u32[]{:S(2)}) collective-permute-start(bf16[2,88,1024]{2,1,0:T(8,128)(2,1)S(1)} %pad_maximum_fusion.10), channel_id=1, source_target_pairs={{0,1},{1,0},{2,3},{3,2},{4,5},{5,4},{6,7},{7,6},{8,9},{9,8},{10,11... | collective-permute-start | bytes 1081352 | tf_op jit(solution)/shard_map/ppermute | solution.py:875
  338.7 48.2 %collective-permute-start.39 = (bf16[2,2,128,768]{3,2,1,0:T(8,128)(2,1)}, bf16[2,2,128,768]{3,2,1,0:T(8,128)(2,1)}, u32[]{:S(2)}, u32[]{:S(2)}) collective-permute-start(bf16[2,2,128,768]{3,2,1,0:T(8,128)(2,1)} %pad_maximum_fusion.6), channel_id=1, source_target_pairs={{0,2},{1,3},{2,0},{3,1},{4,6},{5,7},{6,4},{7,5},{8,10},{9,11},{10,... | collective-permute-start | bytes 2359304 | tf_op jit(solution)/shard_map/ppermute | solution.py:878
  367.5 56.0 %collective-permute-start.48 = (bf16[2,88,1024]{2,1,0:T(8,128)(2,1)}, bf16[2,88,1024]{2,1,0:T(8,128)(2,1)}, u32[]{:S(2)}, u32[]{:S(2)}) collective-permute-start(bf16[2,88,1024]{2,1,0:T(8,128)(2,1)} %pad_maximum_fusion.11), channel_id=1, source_target_pairs={{0,2},{1,3},{2,0},{3,1},{4,6},{5,7},{6,4},{7,5},{8,10},{9,11},{10,... | collective-permute-start | bytes 1081352 | tf_op jit(solution)/shard_map/ppermute | solution.py:878
  380.9 50.7 %collective-permute-start.40 = (bf16[2,8,32,1024]{3,2,1,0:T(8,128)(2,1)}, bf16[2,8,32,1024]{3,2,1,0:T(8,128)(2,1)}, u32[]{:S(2)}, u32[]{:S(2)}) collective-permute-start(bf16[2,8,32,1024]{3,2,1,0:T(8,128)(2,1)} %pad_maximum_fusion.3), channel_id=1, source_target_pairs={{0,1},{1,0},{2,3},{3,2},{4,5},{5,4},{6,7},{7,6},{8,9},{9,8},{10,11... | collective-permute-start | bytes 3145736 | tf_op jit(solution)/shard_map/ppermute | solution.py:875
  (67 other events, 846.3 us)
Sparse Core Ops, SparseCore 0:
  10.1 79.8 all-gather.2
  92.2 151.8 all-gather.4
